TPU v7x, 512 devices: a whole 4x8x8 slice. The times are simulated.
512 devices in a mesh: vocab: 64 (over x, z, core), rep: 8 (over y).
Axes of the slice: x: 4, y: 8, z: 8, core: 2. Of those that a mesh axis runs over, the one named last changes fastest.
Arguments:
- token_ids: int32 [65536], P(('vocab', 'rep')), may hold values from 0 to 8191, as said below
- cotangent: bfloat16 [65536, 4608], P(('vocab', 'rep')), may hold values from -0.059814453 to 0.059814453
- embed_table: bfloat16 [8192, 4608], P('vocab'), may hold values from -0.36 to 0.36
- norm_gain: float32 [4608], replicated, may hold values from 0.1 to 1.9
- moment_one: float32 [8192, 4608], P(('vocab', 'rep')), may hold values from -3 to 3
- moment_two: float32 [8192, 4608], P(('vocab', 'rep')), may hold values from 0.05 to 5
Outputs:
- new_table: bfloat16 [8192, 4608], P('vocab')
- new_moment_one: float32 [8192, 4608], P(('vocab', 'rep'))
- new_moment_two: float32 [8192, 4608], P(('vocab', 'rep'))
Inputs may be any that keep to these rules, and one draw needn't show every extreme that they name: `token_ids`: the ids of one device fall at most 4 times into each vocabulary shard (ids s * 128 to (s + 1) * 128 - 1); in every draw some shard receives exactly 4 ids from every device.
All inputs are finite; a program needn't handle non-finite values.
Results may differ from a plain program's by a relative error of at most 0.003.
Values may be sent and summed in bfloat16 or wider, within the bound.
No kernel may reach another device: no remote copies, remote signals or barrier semaphores. Data moves between devices by JAX's collectives and lax.ppermute only.
A program may use at most 64 MiB of HBM per device.

v0:
```python
import math

import jax
import jax.numpy as jnp
from jax import lax
from jax.sharding import PartitionSpec as P

beta_one = 0.9
beta_two = 0.95
learn_rate = 0.01
decay_rate = 0.01
adam_eps = 1e-08
norm_eps = 1e-06
correct_one = 0.9999734386011124
correct_two = 0.9940794707920236


def token_grads(fetched_rows, cotangent, norm_gain):
    width = fetched_rows.shape[-1]
    root = math.sqrt(width)
    scaled = fetched_rows.astype(jnp.float32) * root
    weighted = cotangent.astype(jnp.float32) * norm_gain
    mean_square = jnp.mean(scaled * scaled, axis=-1, keepdims=True)
    inverse = lax.rsqrt(mean_square + norm_eps)
    inner_mean = jnp.mean(scaled * weighted, axis=-1, keepdims=True)
    return (root * inverse * (weighted - scaled * inverse * inverse * inner_mean)).astype(
        jnp.bfloat16
    )


def lookup(wanted, embed_table):
    shard_rows = embed_table.shape[0]
    picks = (wanted[:, None] == jnp.arange(shard_rows, dtype=jnp.int32)[None, :]).astype(
        jnp.bfloat16
    )
    return jnp.dot(picks, embed_table, preferred_element_type=jnp.float32).astype(jnp.bfloat16)


def accumulate(wanted, token_grad, shard_rows):
    picks = (jnp.arange(shard_rows, dtype=jnp.int32)[:, None] == wanted[None, :]).astype(
        jnp.bfloat16
    )
    return jnp.dot(picks, token_grad, preferred_element_type=jnp.float32)


def on_device(token_ids, cotangent, embed_table, norm_gain, moment_one, moment_two):
    shard_rows = embed_table.shape[0]
    width = embed_table.shape[1]
    tok_count = token_ids.shape[0]
    peer_count = lax.axis_size("vocab")
    capacity = max(2, 2 * tok_count // peer_count)
    owner_index = token_ids // shard_rows
    local_row = token_ids - owner_index * shard_rows
    owner_hits = (owner_index[:, None] == jnp.arange(peer_count, dtype=jnp.int32)[None, :]).astype(
        jnp.int32
    )
    position = jnp.sum((jnp.cumsum(owner_hits, axis=0) - 1) * owner_hits, axis=1)
    slot_index = owner_index * capacity + position
    requests = jnp.full((peer_count * capacity,), -1, jnp.int32).at[slot_index].set(local_row)
    incoming = lax.all_to_all(requests, "vocab", split_axis=0, concat_axis=0, tiled=True)
    fetched_rows = lookup(incoming, embed_table)
    returned = lax.all_to_all(fetched_rows, "vocab", split_axis=0, concat_axis=0, tiled=True)
    token_grad = token_grads(returned[slot_index], cotangent, norm_gain)
    outgoing = (
        jnp.zeros((peer_count * capacity, width), jnp.bfloat16).at[slot_index].set(token_grad)
    )
    arrived = lax.all_to_all(outgoing, "vocab", split_axis=0, concat_axis=0, tiled=True)
    row_grad = accumulate(incoming, arrived, shard_rows)
    slice_grad = lax.psum_scatter(row_grad, "rep", scatter_dimension=0, tiled=True)
    slice_rows = slice_grad.shape[0]
    own_rows = lax.dynamic_slice_in_dim(
        embed_table, lax.axis_index("rep") * slice_rows, slice_rows, 0
    )
    new_moment_one = beta_one * moment_one + (1.0 - beta_one) * slice_grad
    new_moment_two = beta_two * moment_two + (1.0 - beta_two) * slice_grad * slice_grad
    params = own_rows.astype(jnp.float32)
    update = (
        new_moment_one / correct_one / (jnp.sqrt(new_moment_two / correct_two) + adam_eps)
        + decay_rate * params
    )
    updated = (params - learn_rate * update).astype(jnp.bfloat16)
    new_table = lax.all_gather(updated, "rep", axis=0, tiled=True)
    return (new_table, new_moment_one, new_moment_two)


def solution(mesh):
    placed = (
        P(("vocab", "rep")),
        P(("vocab", "rep"), None),
        P("vocab", None),
        P(),
        P(("vocab", "rep"), None),
        P(("vocab", "rep"), None),
    )
    return jax.shard_map(
        on_device,
        mesh=mesh,
        in_specs=placed,
        out_specs=(P("vocab", None), P(("vocab", "rep"), None), P(("vocab", "rep"), None)),
        check_vma=False,
    )
```

profile of v0, /device:TPU:6, one launch (start us, length us, event | category | flops | bytes accessed | tf_op | source)
XLA Modules:
  0.0 275.4 jit_solution(2908983757643015907)
XLA Ops:
  7.2 0.7 multiply_subtract_fusion
  7.9 0.2 reduce_window_sum.11
  8.1 0.2 select_reduce_fusion
  8.3 1.0 scatter_custom_fusion
  9.4 21.4 %all_to_all.33 = s32[64,4,1]{1,2,0:T(1,128)S(1)} all-to-all(s32[64,4,1]{1,2,0:T(1,128)S(1)} %bitcast.4), channel_id=1, replica_groups=mesh['vocab'=64,'rep'=8] {'vocab'}, dimensions={0} | all-to-all | bytes 2048 | tf_op jit(solution)/shard_map/all_to_all | solution.py:60
  30.8 0.5 broadcast.84
  31.3 0.7 reduce.3
  32.0 0.1 eq.45
  32.1 2.1 convolution_convert_fusion
  34.2 2.1 all_to_all.24
  36.3 7.4 %all-to-all-start.1 = ((bf16[64,4,4608]{2,1,0:T(4,128)(2,1)}), bf16[64,4,4608]{2,1,0:T(4,128)(2,1)}, u32[]{:S(2)}, u32[]{:S(2)}) async-start(bf16[64,4,4608]{2,1,0:T(4,128)(2,1)} %all_to_all.24), calls=%async_computation.1 | async-start | bytes 4718592 | tf_op jit(solution)/shard_map/all_to_all | solution.py:62
  43.8 54.1 %all-to-all-done.1 = bf16[64,4,4608]{2,1,0:T(4,128)(2,1)} async-done(((bf16[64,4,4608]{2,1,0:T(4,128)(2,1)}), bf16[64,4,4608]{2,1,0:T(4,128)(2,1)}, u32[]{:S(2)}, u32[]{:S(2)}) %all-to-all-start.1) | async-done | bytes 2359328 | tf_op jit(solution)/shard_map/all_to_all | solution.py:62
  97.9 2.6 all_to_all.26
  100.5 1.3 gather_fusion
  101.8 2.0 fusion.2
  103.8 4.2 %scatter_custom_fusion.1 = bf16[256,4608]{1,0:T(8,128)(2,1)S(1)} fusion(s32[128]{0:T(128)} %copy-done.2, bf16[128,4608]{1,0:T(8,128)(2,1)S(1)} %gather_fusion, bf16[128,4608]{1,0:T(8,128)(2,1)} %param.7, f32[128]{0:T(128)S(1)} %get-tuple-element.12, f32[128]{0:T(128)S(1)} %get-tuple-element.11, f32[4608]{0:T(1024)} %param.9, f32[128]{0:T(128)S(1)} %get-tuple-element.10, ...), kind=kCustom, calls=%fused_computation.16 | custom fusion | flops 5308416 | bytes 4741120 | tf_op jit(solution)/shard_map/scatter | solution.py:65
  108.1 2.1 all_to_all.27
  110.2 65.1 %all_to_all.34 = bf16[64,4,4608]{2,1,0:T(4,128)(2,1)} all-to-all(bf16[64,4,4608]{2,1,0:T(4,128)(2,1)} %all_to_all.27), channel_id=1, replica_groups=mesh['vocab'=64,'rep'=8] {'vocab'}, dimensions={0} | all-to-all | bytes 4718592 | tf_op jit(solution)/shard_map/all_to_all | solution.py:67
  175.3 2.6 all_to_all.29
  177.9 1.9 fusion.20
  179.9 42.5 %reduce-scatter.2.cloned.1.call-done = f32[16,4608]{1,0:T(8,128)} async-done(((f32[128,4608]{1,0:T(8,128)}), f32[16,4608]{1,0:T(8,128)}) %reduce-scatter.2.cloned.1.call-update) | async-done | bytes 294928 | tf_op jit(solution)/shard_map/reduce_scatter | solution.py:69
  222.4 2.0 fusion.18
  224.5 41.7 %all-gather.2.cloned.1.call-done = bf16[128,4608]{1,0:T(8,128)(2,1)} async-done(((bf16[16,4608]{1,0:T(8,128)(2,1)}), bf16[128,4608]{1,0:T(8,128)(2,1)}) %all-gather.2.cloned.1.call-update) | async-done | bytes 1179664 | tf_op jit(solution)/shard_map/all_gather | solution.py:82
  266.2 2.4 copy.11
  (15 shorter events, 0.3 us)
Async XLA Ops:
  8.3 35.5 %copy-start.2 = (s32[128]{0:T(128)}, s32[128]{0:T(128)S(1)}, u32[]{:S(2)}) copy-start(s32[128]{0:T(128)S(1)} %compare_select_fusion) | copy-start | bytes 1540
  36.3 61.6 %all-to-all-start.1 = ((bf16[64,4,4608]{2,1,0:T(4,128)(2,1)}), bf16[64,4,4608]{2,1,0:T(4,128)(2,1)}, u32[]{:S(2)}, u32[]{:S(2)}) async-start(bf16[64,4,4608]{2,1,0:T(4,128)(2,1)} %all_to_all.24), calls=%async_computation.1 | async-start | bytes 4718592 | tf_op jit(solution)/shard_map/all_to_all | solution.py:62
  43.7 178.7 %reduce-scatter.2.cloned.1.call-start = ((), (), s32[]{:S(2)}) async-start(), calls=%async_computation.4 | async-start | bytes 2654208 | tf_op jit(solution)/shard_map/reduce_scatter | solution.py:69
  179.8 42.6 %copy-start = (f32[16,4608]{1,0:T(8,128)S(1)}, f32[16,4608]{1,0:T(8,128)}, u32[]{:S(2)}) copy-start(f32[16,4608]{1,0:T(8,128)} %param.10) | copy-start | bytes 884740
  179.8 42.6 %copy-start.1 = (f32[16,4608]{1,0:T(8,128)S(1)}, f32[16,4608]{1,0:T(8,128)}, u32[]{:S(2)}) copy-start(f32[16,4608]{1,0:T(8,128)} %param.11) | copy-start | bytes 884740
  179.8 86.3 %all-gather.2.cloned.1.call-start = ((), (), s32[]{:S(2)}) async-start(), calls=%async_computation.5 | async-start | bytes 1327104 | tf_op jit(solution)/shard_map/all_gather | solution.py:82
Sparse Core Ops, SparseCore 0:
  180.0 42.4 reduce-scatter.1
  225.1 41.0 all-gather.1
where the time goes:
time: 276 us; the launch traced here: 275 us
  waiting for transfers between devices  138 us (50%)
  blocking collectives  86.5 us (31%)
  local copies, waits for them, and re-layouts  14.9 us (5%)
  between operations  14.2 us (5%)
  other arithmetic  10.1 us (4%)
  starting transfers between devices  7.48 us (3%)
  matrix products  3.98 us (1%)
    all_to_all x1, blocking collectives, on_device(): lax.all_to_all(outgoing, 'vocab', split_axis=0, concat_axis=0, tiled=True)  65.1 us
    all_to_all x1, waiting for transfers between devices, on_device(): lax.all_to_all(fetched_rows, 'vocab', split_axis=0, concat_axis=0, tiled=...  54.1 us
    reduce_scatter x1, waiting for transfers between devices, on_device(): lax.psum_scatter(row_grad, 'rep', scatter_dimension=0, tiled=True)  42.5 us
    all_gather x1, waiting for transfers between devices, on_device(): new_table = lax.all_gather(updated, 'rep', axis=0, tiled=True)  41.7 us
    all_to_all x1, blocking collectives, on_device(): lax.all_to_all(requests, 'vocab', split_axis=0, concat_axis=0, tiled=True)  21.4 us
    all_to_all x1, starting transfers between devices, on_device(): lax.all_to_all(fetched_rows, 'vocab', split_axis=0, concat_axis=0, tiled=...  7.4 us
  transfers between devices with their start and end apart: 3, of which 3 were waited for; matrix products, arithmetic and copies ran while one was open for 0% of the time, Pallas kernels for 0%

commit v1 on v0

v1 whole, which is shorter than its diff:
```python
import math

import jax
import jax.numpy as jnp
from jax import lax
from jax.experimental import pallas as pl
from jax.experimental.pallas import tpu as pltpu
from jax.sharding import PartitionSpec as P

beta_one = 0.9
beta_two = 0.95
learn_rate = 0.01
decay_rate = 0.01
adam_eps = 1e-08
norm_eps = 1e-06
correct_one = 0.9999734386011124
correct_two = 0.9940794707920236

SLOTS = 4
LANES = 128
GATHERED = 3968


def pack_body(ids_ref, cot_ref, out_ref):
    tok_count, width = cot_ref.shape
    half = width // 2
    block_rows = out_ref.shape[0]
    ids_along = jnp.broadcast_to(ids_ref[...], (tok_count, tok_count))
    ids_down = ids_along.T
    down = lax.broadcasted_iota(jnp.int32, (tok_count, tok_count), 0)
    along = lax.broadcasted_iota(jnp.int32, (tok_count, tok_count), 1)
    earlier = ((ids_along >> 7) == (ids_down >> 7)) & (down < along)
    position = jnp.sum(earlier.astype(jnp.int32), axis=0, keepdims=True)
    slot = (ids_ref[...] >> 7) * (2 * SLOTS) + position
    slots = jnp.concatenate([slot, slot + SLOTS], axis=1)
    rows = lax.broadcasted_iota(jnp.int32, (block_rows, 2 * tok_count), 0)
    rows = rows + pl.program_id(0) * block_rows
    picks = (rows == slots).astype(jnp.bfloat16)
    halves = jnp.concatenate([cot_ref[:, :half], cot_ref[:, half:]], axis=0)
    out_ref[:, :half] = jnp.dot(picks, halves, preferred_element_type=jnp.float32).astype(
        jnp.bfloat16
    )
    marks = ((ids_down & (LANES - 1)) == along).astype(jnp.bfloat16)
    marks = jnp.concatenate([marks, marks], axis=0)
    out_ref[:, half:] = jnp.dot(picks, marks, preferred_element_type=jnp.float32).astype(
        jnp.bfloat16
    )


def pack(token_ids, cotangent, peer_count):
    tok_count, width = cotangent.shape
    lanes = width // 2 + LANES
    rows = peer_count * 2 * SLOTS
    steps = 4
    return pl.pallas_call(
        pack_body,
        grid=(steps,),
        in_specs=[
            pl.BlockSpec((1, tok_count), lambda i: (0, 0)),
            pl.BlockSpec((tok_count, width), lambda i: (0, 0)),
        ],
        out_specs=pl.BlockSpec((rows // steps, lanes), lambda i: (i, 0)),
        out_shape=jax.ShapeDtypeStruct((rows, lanes), jnp.bfloat16),
        compiler_params=pltpu.CompilerParams(vmem_limit_bytes=40 * 1024 * 1024),
        cost_estimate=pl.CostEstimate(
            flops=2 * rows * 2 * tok_count * lanes,
            bytes_accessed=2 * (tok_count * width + rows * lanes),
            transcendentals=0,
        ),
        name="pack",
    )(token_ids.reshape(1, tok_count), cotangent)


def collect_body(marks_ref, part_ref, out_ref):
    count, part = part_ref.shape
    half = out_ref.shape[1] // 2
    which = lax.broadcasted_iota(jnp.int32, (count, LANES), 0) & SLOTS
    marks = marks_ref[...].astype(jnp.float32)
    first = jnp.where(which == 0, marks, 0.0)
    second = jnp.where(which == 0, 0.0, marks)
    picks = jnp.concatenate([first.T, second.T], axis=0).astype(jnp.bfloat16)
    sums = jnp.dot(picks, part_ref[...], preferred_element_type=jnp.float32)
    at = pl.multiple_of(pl.program_id(0) * part, LANES)
    out_ref[:, pl.ds(at, part)] = sums[:LANES]
    out_ref[:, pl.ds(half + at, part)] = sums[LANES:]


def collect(arrived):
    count, lanes = arrived.shape
    half = lanes - LANES
    steps = 3
    part = half // steps
    return pl.pallas_call(
        collect_body,
        grid=(steps,),
        in_specs=[
            pl.BlockSpec((count, LANES), lambda i: (0, half // LANES)),
            pl.BlockSpec((count, part), lambda i: (0, i)),
        ],
        out_specs=pl.BlockSpec((LANES, 2 * half), lambda i: (0, 0)),
        out_shape=jax.ShapeDtypeStruct((LANES, 2 * half), jnp.float32),
        compiler_params=pltpu.CompilerParams(vmem_limit_bytes=40 * 1024 * 1024),
        cost_estimate=pl.CostEstimate(
            flops=2 * count * 2 * LANES * half,
            bytes_accessed=2 * count * lanes + 8 * LANES * half,
            transcendentals=0,
        ),
        name="collect",
    )(arrived, arrived)


def adam_body(rep_ref, sum_ref, table_ref, gain_ref, one_ref, two_ref, up_ref, rest_ref, one_out, two_out):
    width = sum_ref.shape[1]
    root = math.sqrt(width)
    params = table_ref[...].astype(jnp.float32)
    scaled = params * root
    weighted = sum_ref[...] * gain_ref[...]
    mean_square = jnp.mean(scaled * scaled, axis=-1, keepdims=True)
    inverse = lax.rsqrt(mean_square + norm_eps)
    inner_mean = jnp.mean(scaled * weighted, axis=-1, keepdims=True)
    grad = root * inverse * (weighted - scaled * (inverse * inverse * inner_mean))
    new_one = beta_one * one_ref[...] + (1.0 - beta_one) * grad
    new_two = beta_two * two_ref[...] + (1.0 - beta_two) * grad * grad
    one_out[...] = new_one
    two_out[...] = new_two
    update = (
        new_one / correct_one / (jnp.sqrt(new_two / correct_two) + adam_eps) + decay_rate * params
    )
    updated = (params - learn_rate * update).astype(jnp.bfloat16)
    up_ref[...] = updated[:, :GATHERED]
    rest = updated[:, GATHERED:]
    rows = rest.shape[0]
    for peer in range(rest_ref.shape[0] // rows):
        rest_ref[peer * rows : (peer + 1) * rows, :] = rest


def adam(rep_index, slice_sum, embed_table, norm_gain, moment_one, moment_two):
    rows, width = slice_sum.shape
    peers = embed_table.shape[0] // rows
    whole = pl.BlockSpec((rows, width), lambda i, rep: (0, 0))
    return pl.pallas_call(
        adam_body,
        grid_spec=pltpu.PrefetchScalarGridSpec(
            num_scalar_prefetch=1,
            grid=(1,),
            in_specs=[
                whole,
                pl.BlockSpec((rows, width), lambda i, rep: (rep[0], 0)),
                pl.BlockSpec((1, width), lambda i, rep: (0, 0)),
                whole,
                whole,
            ],
            out_specs=[
                pl.BlockSpec((rows, GATHERED), lambda i, rep: (0, 0)),
                pl.BlockSpec((peers * rows, width - GATHERED), lambda i, rep: (0, 0)),
                whole,
                whole,
            ],
        ),
        out_shape=[
            jax.ShapeDtypeStruct((rows, GATHERED), jnp.bfloat16),
            jax.ShapeDtypeStruct((peers * rows, width - GATHERED), jnp.bfloat16),
            jax.ShapeDtypeStruct((rows, width), jnp.float32),
            jax.ShapeDtypeStruct((rows, width), jnp.float32),
        ],
        compiler_params=pltpu.CompilerParams(vmem_limit_bytes=40 * 1024 * 1024),
        cost_estimate=pl.CostEstimate(
            flops=40 * rows * width, bytes_accessed=24 * rows * width, transcendentals=rows * width
        ),
        name="adam",
    )(rep_index, slice_sum, embed_table, norm_gain.reshape(1, width), moment_one, moment_two)


def on_device(token_ids, cotangent, embed_table, norm_gain, moment_one, moment_two):
    peer_count = lax.axis_size("vocab")
    outgoing = pack(token_ids, cotangent, peer_count)
    arrived = lax.all_to_all(outgoing, "vocab", split_axis=0, concat_axis=0, tiled=True)
    row_sum = collect(arrived)
    slice_sum = lax.psum_scatter(row_sum, "rep", scatter_dimension=0, tiled=True)
    rep_index = lax.axis_index("rep").astype(jnp.int32).reshape(1)
    updated, rest, new_moment_one, new_moment_two = adam(
        rep_index, slice_sum, embed_table, norm_gain, moment_one, moment_two
    )
    left = lax.all_gather(updated, "rep", axis=0, tiled=True)
    right = lax.all_to_all(rest, "rep", split_axis=0, concat_axis=0, tiled=True)
    new_table = jnp.concatenate([left, right], axis=1)
    return (new_table, new_moment_one, new_moment_two)


def solution(mesh):
    placed = (
        P(("vocab", "rep")),
        P(("vocab", "rep"), None),
        P("vocab", None),
        P(),
        P(("vocab", "rep"), None),
        P(("vocab", "rep"), None),
    )
    return jax.shard_map(
        on_device,
        mesh=mesh,
        in_specs=placed,
        out_specs=(P("vocab", None), P(("vocab", "rep"), None), P(("vocab", "rep"), None)),
        check_vma=False,
    )
```

time: 276 us -> 174 us (0.63)
  waiting for transfers between devices: 138 us -> 42.1 us
  blocking collectives: 86.5 us -> 101 us
  local copies, waits for them, and re-layouts: 14.9 us -> 3.59 us
  other arithmetic: 10.1 us -> 1.1 us
  Pallas kernels: 0 us -> 6.04 us
  matrix products: 3.98 us -> 0 us
    all_to_all x1, waiting for transfers between devices: 54.1 us -> 0.01 us  [on_device(): right = lax.all_to_all(rest, 'rep', split_axis=0, concat_axis=0, tiled=True)]
    all_gather x1 -> x0, waiting for transfers between devices: 41.7 us -> none  [on_device(): new_table = lax.all_gather(updated, 'rep', axis=0, tiled=True)]
    all_gather x0 -> x1, blocking collectives: none -> 28.6 us  [on_device(): left = lax.all_gather(updated, 'rep', axis=0, tiled=True)]
    all_to_all x1 -> x0, blocking collectives: 21.4 us -> none  [on_device(): lax.all_to_all(requests, 'vocab', split_axis=0, concat_axis=0, tiled=True)]
    all_to_all x6 -> x0, local copies, waits for them, and re-layouts: 10.1 us -> none  [the longest x2 4.78 us: on_device(): lax.all_to_all(outgoing, 'vocab', split_axis=0, concat_axis=0, tiled=True)]
    all_to_all x1, blocking collectives: 65.1 us -> 72.9 us  [on_device(): lax.all_to_all(outgoing, 'vocab', split_axis=0, concat_axis=0, tiled=True)]
    pallas_call x0 -> x3, Pallas kernels: none -> 6.04 us  [the longest x1 3.01 us: collect(): pl.pallas_call(collect_body, grid=(steps,), in_specs=[pl.BlockSpec((count...]
    scatter x1 -> x0, other arithmetic: 4.24 us -> none  [on_device(): jnp.zeros((peer_count * capacity, width), jnp.bfloat16).at[slot_index]]
  transfers between devices with their start and end apart: 3 -> 2, of which waited for: 3 -> 1; matrix products, arithmetic and copies ran while one was open for 0% -> 0% of each run, Pallas kernels for 0% -> 0%
where the time goes in v1:
time: 174 us
  blocking collectives  101 us (58%)
  waiting for transfers between devices  42.1 us (24%)
  between operations  14.1 us (8%)
  Pallas kernels  6.04 us (3%)
  starting transfers between devices  5.17 us (3%)
  local copies, waits for them, and re-layouts  3.59 us (2%)
    all_to_all x1, blocking collectives, on_device(): lax.all_to_all(outgoing, 'vocab', split_axis=0, concat_axis=0, tiled=True)  72.9 us
    reduce_scatter x1, waiting for transfers between devices, on_device(): lax.psum_scatter(row_sum, 'rep', scatter_dimension=0, tiled=True)  42.1 us
    all_gather x1, blocking collectives, on_device(): left = lax.all_gather(updated, 'rep', axis=0, tiled=True)  28.6 us
    all_to_all x1, starting transfers between devices, on_device(): right = lax.all_to_all(rest, 'rep', split_axis=0, concat_axis=0, tiled=True)  5.14 us
    unnamed x14, local copies, waits for them, and re-layouts  3.58 us
  transfers between devices with their start and end apart: 2, of which 1 were waited for; matrix products, arithmetic and copies ran while one was open for 0% of the time, Pallas kernels for 0%

profile of v1, /device:TPU:6, one launch (start us, length us, event | category | flops | bytes accessed | tf_op | source)
XLA Modules:
  0.0 173.5 jit_solution(17988554943065856163)
XLA Ops:
  7.2 0.0 reduce-scatter.2.cloned.1.call-start
  7.2 0.0 copy-start.1
  7.2 1.3 copy-done.1
  8.5 0.0 copy-start.5
  8.5 0.7 copy-done.5
  9.1 1.7 pack.1
  10.9 72.9 %all_to_all.23 = bf16[64,8,2432]{2,1,0:T(8,128)(2,1)S(1)} all-to-all(bf16[64,8,2432]{2,1,0:T(8,128)(2,1)S(1)} %bitcast.8), channel_id=1, replica_groups=mesh['vocab'=64,'rep'=8] {'vocab'}, dimensions={0} | all-to-all | bytes 4980736 | tf_op jit(solution)/shard_map/all_to_all | solution.py:177
  83.8 3.0 %collect.1 = f32[128,4608]{1,0:T(8,128)} custom-call(bf16[512,2432]{1,0:T(8,128)(2,1)S(1)} %bitcast.6, bf16[512,2432]{1,0:T(8,128)(2,1)S(1)} %bitcast.7), custom_call_target="tpu_custom_call" | custom-call | flops 603979776 | bytes 4849664 | tf_op jit(solution)/shard_map/collect/pallas_call | solution.py:93
  86.8 0.0 copy-start.6
  86.8 0.0 copy-start
  86.8 0.0 copy-start.2
  86.8 0.0 copy-start.3
  86.8 0.0 reduce-scatter.2.cloned.1.call-update
  86.8 0.7 copy-done.6
  87.5 42.1 %reduce-scatter.2.cloned.1.call-done.sum_ref = f32[16,4608]{1,0:T(8,128)} async-done(((f32[128,4608]{1,0:T(8,128)}), f32[16,4608]{1,0:T(8,128)}) %reduce-scatter.2.cloned.1.call-update) | async-done | bytes 294928 | tf_op jit(solution)/shard_map/reduce_scatter | solution.py:179
  129.6 0.0 copy-done
  129.6 0.0 copy-done.2
  129.6 0.0 copy-done.3
  129.7 1.0 copy-done.4
  130.6 1.3 adam.1
  131.9 5.1 %all-to-all-start.1 = ((bf16[8,16,640]{2,1,0:T(8,128)(2,1)}), bf16[8,16,640]{2,1,0:T(8,128)(2,1)S(1)}, u32[]{:S(2)}, u32[]{:S(2)}) async-start(bf16[8,16,640]{2,1,0:T(8,128)(2,1)} %bitcast.4), calls=%async_computation.2 | async-start | bytes 327680 | tf_op jit(solution)/shard_map/all_to_all | solution.py:185
  137.0 28.6 %all_gather.3 = bf16[128,3968]{1,0:T(8,128)(2,1)S(1)} all-gather(bf16[16,3968]{1,0:T(8,128)(2,1)S(1)} %get-tuple-element.7), channel_id=1, replica_groups=mesh['vocab'=64,'rep'=8] {'rep'}, dimensions={0}, use_global_device_ids=true | all-gather | bytes 1142784 | tf_op jit(solution)/shard_map/all_gather | solution.py:184
  165.6 0.0 all-to-all-done.1
  165.6 1.1 pad_maximum_fusion
  (2 shorter events, 0.0 us)
Async XLA Ops:
  7.2 122.5 %reduce-scatter.2.cloned.1.call-start = ((), (), s32[]{:S(2)}) async-start(), calls=%async_computation.3 | async-start | bytes 2654208 | tf_op jit(solution)/shard_map/reduce_scatter | solution.py:179
  7.2 1.3 copy-start.1
  8.5 0.7 copy-start.5
  86.8 0.7 copy-start.6
  86.8 42.9 %copy-start = (bf16[128,4608]{1,0:T(8,128)(2,1)S(1)}, bf16[128,4608]{1,0:T(8,128)(2,1)}, u32[]{:S(2)}) copy-start(bf16[128,4608]{1,0:T(8,128)(2,1)} %table_ref.1) | copy-start | bytes 3538948
  86.8 42.9 %copy-start.2 = (f32[16,4608]{1,0:T(8,128)S(1)}, f32[16,4608]{1,0:T(8,128)}, u32[]{:S(2)}) copy-start(f32[16,4608]{1,0:T(8,128)} %one_ref.1) | copy-start | bytes 884740
  86.8 42.9 %copy-start.3 = (f32[16,4608]{1,0:T(8,128)S(1)}, f32[16,4608]{1,0:T(8,128)}, u32[]{:S(2)}) copy-start(f32[16,4608]{1,0:T(8,128)} %two_ref.1) | copy-start | bytes 884740
  129.6 1.0 copy-start.4
  131.9 33.7 %all-to-all-start.1 = ((bf16[8,16,640]{2,1,0:T(8,128)(2,1)}), bf16[8,16,640]{2,1,0:T(8,128)(2,1)S(1)}, u32[]{:S(2)}, u32[]{:S(2)}) async-start(bf16[8,16,640]{2,1,0:T(8,128)(2,1)} %bitcast.4), calls=%async_computation.2 | async-start | bytes 327680 | tf_op jit(solution)/shard_map/all_to_all | solution.py:185
Sparse Core Ops, SparseCore 0:
  86.9 42.6 reduce-scatter.1

commit v2 on v1

--- a/solution.py
+++ b/solution.py
@@ -79,7 +79,7 @@
     first = jnp.where(which == 0, marks, 0.0)
     second = jnp.where(which == 0, 0.0, marks)
     picks = jnp.concatenate([first.T, second.T], axis=0).astype(jnp.bfloat16)
-    sums = jnp.dot(picks, part_ref[...], preferred_element_type=jnp.float32)
+    sums = jnp.dot(picks, part_ref[...], preferred_element_type=jnp.float32).astype(jnp.bfloat16)
     at = pl.multiple_of(pl.program_id(0) * part, LANES)
     out_ref[:, pl.ds(at, part)] = sums[:LANES]
     out_ref[:, pl.ds(half + at, part)] = sums[LANES:]
@@ -98,11 +98,11 @@
             pl.BlockSpec((count, part), lambda i: (0, i)),
         ],
         out_specs=pl.BlockSpec((LANES, 2 * half), lambda i: (0, 0)),
-        out_shape=jax.ShapeDtypeStruct((LANES, 2 * half), jnp.float32),
+        out_shape=jax.ShapeDtypeStruct((LANES, 2 * half), jnp.bfloat16),
         compiler_params=pltpu.CompilerParams(vmem_limit_bytes=40 * 1024 * 1024),
         cost_estimate=pl.CostEstimate(
             flops=2 * count * 2 * LANES * half,
-            bytes_accessed=2 * count * lanes + 8 * LANES * half,
+            bytes_accessed=2 * count * lanes + 4 * LANES * half,
             transcendentals=0,
         ),
         name="collect",
@@ -114,7 +114,11 @@
     root = math.sqrt(width)
     params = table_ref[...].astype(jnp.float32)
     scaled = params * root
-    weighted = sum_ref[...] * gain_ref[...]
+    rows = table_ref.shape[0]
+    total = sum_ref[:rows, :].astype(jnp.float32)
+    for peer in range(1, sum_ref.shape[0] // rows):
+        total = total + sum_ref[peer * rows : (peer + 1) * rows, :].astype(jnp.float32)
+    weighted = total * gain_ref[...]
     mean_square = jnp.mean(scaled * scaled, axis=-1, keepdims=True)
     inverse = lax.rsqrt(mean_square + norm_eps)
     inner_mean = jnp.mean(scaled * weighted, axis=-1, keepdims=True)
@@ -129,13 +133,12 @@
     updated = (params - learn_rate * update).astype(jnp.bfloat16)
     up_ref[...] = updated[:, :GATHERED]
     rest = updated[:, GATHERED:]
-    rows = rest.shape[0]
     for peer in range(rest_ref.shape[0] // rows):
         rest_ref[peer * rows : (peer + 1) * rows, :] = rest
 
 
-def adam(rep_index, slice_sum, embed_table, norm_gain, moment_one, moment_two):
-    rows, width = slice_sum.shape
+def adam(rep_index, partial_sums, embed_table, norm_gain, moment_one, moment_two):
+    rows, width = moment_one.shape
     peers = embed_table.shape[0] // rows
     whole = pl.BlockSpec((rows, width), lambda i, rep: (0, 0))
     return pl.pallas_call(
@@ -144,7 +147,7 @@
             num_scalar_prefetch=1,
             grid=(1,),
             in_specs=[
-                whole,
+                pl.BlockSpec((peers * rows, width), lambda i, rep: (0, 0)),
                 pl.BlockSpec((rows, width), lambda i, rep: (rep[0], 0)),
                 pl.BlockSpec((1, width), lambda i, rep: (0, 0)),
                 whole,
@@ -168,7 +171,7 @@
             flops=40 * rows * width, bytes_accessed=24 * rows * width, transcendentals=rows * width
         ),
         name="adam",
-    )(rep_index, slice_sum, embed_table, norm_gain.reshape(1, width), moment_one, moment_two)
+    )(rep_index, partial_sums, embed_table, norm_gain.reshape(1, width), moment_one, moment_two)
 
 
 def on_device(token_ids, cotangent, embed_table, norm_gain, moment_one, moment_two):
@@ -176,10 +179,10 @@
     outgoing = pack(token_ids, cotangent, peer_count)
     arrived = lax.all_to_all(outgoing, "vocab", split_axis=0, concat_axis=0, tiled=True)
     row_sum = collect(arrived)
-    slice_sum = lax.psum_scatter(row_sum, "rep", scatter_dimension=0, tiled=True)
+    partial_sums = lax.all_to_all(row_sum, "rep", split_axis=0, concat_axis=0, tiled=True)
     rep_index = lax.axis_index("rep").astype(jnp.int32).reshape(1)
     updated, rest, new_moment_one, new_moment_two = adam(
-        rep_index, slice_sum, embed_table, norm_gain, moment_one, moment_two
+        rep_index, partial_sums, embed_table, norm_gain, moment_one, moment_two
     )
     left = lax.all_gather(updated, "rep", axis=0, tiled=True)
     right = lax.all_to_all(rest, "rep", split_axis=0, concat_axis=0, tiled=True)

time: 174 us -> 155 us (0.89)
  between operations: 14.1 us -> 0.68 us
  waiting for transfers between devices: 42.1 us -> 32.1 us
  starting transfers between devices: 5.17 us -> 10.6 us
    reduce_scatter x1 -> x0, waiting for transfers between devices: 42.1 us -> none  [on_device(): lax.psum_scatter(row_sum, 'rep', scatter_dimension=0, tiled=True)]
    all_to_all x0 -> x1, waiting for transfers between devices: none -> 32.1 us  [on_device(): lax.all_to_all(row_sum, 'rep', split_axis=0, concat_axis=0, tiled=True)]
    all_to_all x0 -> x1, starting transfers between devices: none -> 7.25 us  [on_device(): lax.all_to_all(row_sum, 'rep', split_axis=0, concat_axis=0, tiled=True)]
    all_to_all x1, starting transfers between devices: 5.14 us -> 3.38 us  [on_device(): right = lax.all_to_all(rest, 'rep', split_axis=0, concat_axis=0, tiled=True)]
    unnamed x14 -> x12, local copies, waits for them, and re-layouts: 3.58 us -> 1.93 us
where the time goes in v2:
time: 155 us; the launch traced here: 154 us
  blocking collectives  102 us (66%)
  waiting for transfers between devices  32.1 us (21%)
  starting transfers between devices  10.6 us (7%)
  Pallas kernels  5.76 us (4%)
  local copies, waits for them, and re-layouts  1.95 us (1%)
    all_to_all x1, blocking collectives, on_device(): lax.all_to_all(outgoing, 'vocab', split_axis=0, concat_axis=0, tiled=True)  72.9 us
    all_to_all x1, waiting for transfers between devices, on_device(): lax.all_to_all(row_sum, 'rep', split_axis=0, concat_axis=0, tiled=True)  32.1 us
    all_gather x1, blocking collectives, on_device(): left = lax.all_gather(updated, 'rep', axis=0, tiled=True)  29.2 us
    all_to_all x1, starting transfers between devices, on_device(): lax.all_to_all(row_sum, 'rep', split_axis=0, concat_axis=0, tiled=True)  7.25 us
    all_to_all x1, starting transfers between devices, on_device(): right = lax.all_to_all(rest, 'rep', split_axis=0, concat_axis=0, tiled=True)  3.38 us
  transfers between devices with their start and end apart: 2, of which 1 were waited for; matrix products, arithmetic and copies ran while one was open for 0% of the time, Pallas kernels for 0%

profile of v2, /device:TPU:6, one launch (start us, length us, event | category | flops | bytes accessed | tf_op | source)
XLA Modules:
  0.0 154.3 jit_solution(8385867533099651226)
XLA Ops:
  0.6 0.0 copy-start
  0.6 1.3 copy-done
  1.9 0.0 copy-start.4
  1.9 0.7 copy-done.4
  2.6 1.7 %pack.1 = bf16[512,2432]{1,0:T(8,128)(2,1)S(1)} custom-call(s32[1,128]{1,0:T(1,128)S(1)} %bitcast.12, bf16[128,4608]{1,0:T(8,128)(2,1)S(1)} %copy-done), custom_call_target="tpu_custom_call" | custom-call | flops 637534208 | bytes 3670016 | tf_op jit(solution)/shard_map/pack/pallas_call | solution.py:55
  4.3 72.9 %all_to_all.34 = bf16[64,8,2432]{2,1,0:T(8,128)(2,1)S(1)} all-to-all(bf16[64,8,2432]{2,1,0:T(8,128)(2,1)S(1)} %bitcast.10), channel_id=1, replica_groups=mesh['vocab'=64,'rep'=8] {'vocab'}, dimensions={0} | all-to-all | bytes 4980736 | tf_op jit(solution)/shard_map/all_to_all | solution.py:180
  77.2 2.6 %collect.1 = bf16[128,4608]{1,0:T(8,128)(2,1)} custom-call(bf16[512,2432]{1,0:T(8,128)(2,1)S(1)} %bitcast.8, bf16[512,2432]{1,0:T(8,128)(2,1)S(1)} %bitcast.9), custom_call_target="tpu_custom_call" | custom-call | flops 603979776 | bytes 3670016 | tf_op jit(solution)/shard_map/collect/pallas_call | solution.py:93
  79.8 0.0 copy-start.5
  79.8 0.0 copy-start.1
  79.8 0.0 copy-start.2
  79.8 0.0 copy-start.3
  79.8 7.2 %all-to-all-start.1 = ((bf16[8,16,4608]{2,1,0:T(8,128)(2,1)}), bf16[8,16,4608]{2,1,0:T(8,128)(2,1)S(1)}, u32[]{:S(2)}, u32[]{:S(2)}) async-start(bf16[8,16,4608]{2,1,0:T(8,128)(2,1)} %bitcast.4), calls=%async_computation.1 | async-start | bytes 2359296 | tf_op jit(solution)/shard_map/all_to_all | solution.py:182
  87.1 0.0 copy-done.5
  87.1 32.1 %all-to-all-done.1 = bf16[8,16,4608]{2,1,0:T(8,128)(2,1)S(1)} async-done(((bf16[8,16,4608]{2,1,0:T(8,128)(2,1)}), bf16[8,16,4608]{2,1,0:T(8,128)(2,1)S(1)}, u32[]{:S(2)}, u32[]{:S(2)}) %all-to-all-start.1) | async-done | bytes 1179680 | tf_op jit(solution)/shard_map/all_to_all | solution.py:182
  119.2 0.0 copy-done.1
  119.2 0.0 copy-done.2
  119.2 0.0 copy-done.3
  119.2 1.4 adam.1
  120.6 3.4 %all-to-all-start.2 = ((bf16[8,16,640]{2,1,0:T(8,128)(2,1)}), bf16[8,16,640]{2,1,0:T(8,128)(2,1)S(1)}, u32[]{:S(2)}, u32[]{:S(2)}) async-start(bf16[8,16,640]{2,1,0:T(8,128)(2,1)} %bitcast.6), calls=%async_computation.2 | async-start | bytes 327680 | tf_op jit(solution)/shard_map/all_to_all | solution.py:188
  124.0 29.2 %all_gather.3 = bf16[128,3968]{1,0:T(8,128)(2,1)S(1)} all-gather(bf16[16,3968]{1,0:T(8,128)(2,1)S(1)} %get-tuple-element.7), channel_id=1, replica_groups=mesh['vocab'=64,'rep'=8] {'rep'}, dimensions={0}, use_global_device_ids=true | all-gather | bytes 1142784 | tf_op jit(solution)/shard_map/all_gather | solution.py:187
  153.2 0.0 all-to-all-done.2
  153.2 1.1 pad_maximum_fusion
  (1 shorter events, 0.0 us)
Async XLA Ops:
  0.6 1.3 copy-start
  1.9 0.7 copy-start.4
  79.8 7.3 %copy-start.5 = (f32[4608]{0:T(1024)S(1)}, f32[4608]{0:T(1024)}, u32[]{:S(2)}) copy-start(f32[4608]{0:T(1024)} %param.9) | copy-start | bytes 55300
  79.8 39.4 %copy-start.1 = (bf16[128,4608]{1,0:T(8,128)(2,1)S(1)}, bf16[128,4608]{1,0:T(8,128)(2,1)}, u32[]{:S(2)}) copy-start(bf16[128,4608]{1,0:T(8,128)(2,1)} %table_ref.1) | copy-start | bytes 3538948
  79.8 39.4 %copy-start.2 = (f32[16,4608]{1,0:T(8,128)S(1)}, f32[16,4608]{1,0:T(8,128)}, u32[]{:S(2)}) copy-start(f32[16,4608]{1,0:T(8,128)} %one_ref.1) | copy-start | bytes 884740
  79.8 39.4 %copy-start.3 = (f32[16,4608]{1,0:T(8,128)S(1)}, f32[16,4608]{1,0:T(8,128)}, u32[]{:S(2)}) copy-start(f32[16,4608]{1,0:T(8,128)} %two_ref.1) | copy-start | bytes 884740
  79.8 39.4 %all-to-all-start.1 = ((bf16[8,16,4608]{2,1,0:T(8,128)(2,1)}), bf16[8,16,4608]{2,1,0:T(8,128)(2,1)S(1)}, u32[]{:S(2)}, u32[]{:S(2)}) async-start(bf16[8,16,4608]{2,1,0:T(8,128)(2,1)} %bitcast.4), calls=%async_computation.1 | async-start | bytes 2359296 | tf_op jit(solution)/shard_map/all_to_all | solution.py:182
  120.6 32.6 %all-to-all-start.2 = ((bf16[8,16,640]{2,1,0:T(8,128)(2,1)}), bf16[8,16,640]{2,1,0:T(8,128)(2,1)S(1)}, u32[]{:S(2)}, u32[]{:S(2)}) async-start(bf16[8,16,640]{2,1,0:T(8,128)(2,1)} %bitcast.6), calls=%async_computation.2 | async-start | bytes 327680 | tf_op jit(solution)/shard_map/all_to_all | solution.py:188

commit v3 on v2

--- a/solution.py
+++ b/solution.py
@@ -5,6 +5,7 @@
 from jax import lax
 from jax.experimental import pallas as pl
 from jax.experimental.pallas import tpu as pltpu
+from jax.sharding import Mesh
 from jax.sharding import PartitionSpec as P
 
 beta_one = 0.9
@@ -23,7 +24,7 @@
 
 def pack_body(ids_ref, cot_ref, out_ref):
     tok_count, width = cot_ref.shape
-    half = width // 2
+    quarter = width // 4
     block_rows = out_ref.shape[0]
     ids_along = jnp.broadcast_to(ids_ref[...], (tok_count, tok_count))
     ids_down = ids_along.T
@@ -31,26 +32,26 @@
     along = lax.broadcasted_iota(jnp.int32, (tok_count, tok_count), 1)
     earlier = ((ids_along >> 7) == (ids_down >> 7)) & (down < along)
     position = jnp.sum(earlier.astype(jnp.int32), axis=0, keepdims=True)
-    slot = (ids_ref[...] >> 7) * (2 * SLOTS) + position
-    slots = jnp.concatenate([slot, slot + SLOTS], axis=1)
-    rows = lax.broadcasted_iota(jnp.int32, (block_rows, 2 * tok_count), 0)
+    slot = (ids_ref[...] >> 7) * (4 * SLOTS) + position
+    slots = jnp.concatenate([slot + part * SLOTS for part in range(4)], axis=1)
+    rows = lax.broadcasted_iota(jnp.int32, (block_rows, 4 * tok_count), 0)
     rows = rows + pl.program_id(0) * block_rows
     picks = (rows == slots).astype(jnp.bfloat16)
-    halves = jnp.concatenate([cot_ref[:, :half], cot_ref[:, half:]], axis=0)
-    out_ref[:, :half] = jnp.dot(picks, halves, preferred_element_type=jnp.float32).astype(
-        jnp.bfloat16
-    )
+    quarters = [cot_ref[:, part * quarter : (part + 1) * quarter] for part in range(4)]
+    out_ref[:, :quarter] = jnp.dot(
+        picks, jnp.concatenate(quarters, axis=0), preferred_element_type=jnp.float32
+    ).astype(jnp.bfloat16)
     marks = ((ids_down & (LANES - 1)) == along).astype(jnp.bfloat16)
-    marks = jnp.concatenate([marks, marks], axis=0)
-    out_ref[:, half:] = jnp.dot(picks, marks, preferred_element_type=jnp.float32).astype(
+    marks = jnp.concatenate([marks] * 4, axis=0)
+    out_ref[:, quarter:] = jnp.dot(picks, marks, preferred_element_type=jnp.float32).astype(
         jnp.bfloat16
     )
 
 
 def pack(token_ids, cotangent, peer_count):
     tok_count, width = cotangent.shape
-    lanes = width // 2 + LANES
-    rows = peer_count * 2 * SLOTS
+    lanes = width // 4 + LANES
+    rows = peer_count * 4 * SLOTS
     steps = 4
     return pl.pallas_call(
         pack_body,
@@ -63,7 +64,7 @@
         out_shape=jax.ShapeDtypeStruct((rows, lanes), jnp.bfloat16),
         compiler_params=pltpu.CompilerParams(vmem_limit_bytes=40 * 1024 * 1024),
         cost_estimate=pl.CostEstimate(
-            flops=2 * rows * 2 * tok_count * lanes,
+            flops=2 * rows * 4 * tok_count * lanes,
             bytes_accessed=2 * (tok_count * width + rows * lanes),
             transcendentals=0,
         ),
@@ -110,15 +111,18 @@
 
 
 def adam_body(rep_ref, sum_ref, table_ref, gain_ref, one_ref, two_ref, up_ref, rest_ref, one_out, two_out):
-    width = sum_ref.shape[1]
+    width = table_ref.shape[1]
     root = math.sqrt(width)
     params = table_ref[...].astype(jnp.float32)
     scaled = params * root
     rows = table_ref.shape[0]
-    total = sum_ref[:rows, :].astype(jnp.float32)
-    for peer in range(1, sum_ref.shape[0] // rows):
-        total = total + sum_ref[peer * rows : (peer + 1) * rows, :].astype(jnp.float32)
-    weighted = total * gain_ref[...]
+    totals = []
+    for member in range(2):
+        total = sum_ref[member * rows : (member + 1) * rows, :].astype(jnp.float32)
+        for peer in range(member + 2, sum_ref.shape[0] // rows, 2):
+            total = total + sum_ref[peer * rows : (peer + 1) * rows, :].astype(jnp.float32)
+        totals.append(total)
+    weighted = jnp.concatenate(totals, axis=1) * gain_ref[...]
     mean_square = jnp.mean(scaled * scaled, axis=-1, keepdims=True)
     inverse = lax.rsqrt(mean_square + norm_eps)
     inner_mean = jnp.mean(scaled * weighted, axis=-1, keepdims=True)
@@ -147,7 +151,7 @@
             num_scalar_prefetch=1,
             grid=(1,),
             in_specs=[
-                pl.BlockSpec((peers * rows, width), lambda i, rep: (0, 0)),
+                pl.BlockSpec((peers * rows, width // 2), lambda i, rep: (0, 0)),
                 pl.BlockSpec((rows, width), lambda i, rep: (rep[0], 0)),
                 pl.BlockSpec((1, width), lambda i, rep: (0, 0)),
                 whole,
@@ -174,35 +178,41 @@
     )(rep_index, partial_sums, embed_table, norm_gain.reshape(1, width), moment_one, moment_two)
 
 
+REP = ("four", "pair")
+ALL = ("vocab", "four", "pair")
+
+
 def on_device(token_ids, cotangent, embed_table, norm_gain, moment_one, moment_two):
     peer_count = lax.axis_size("vocab")
     outgoing = pack(token_ids, cotangent, peer_count)
-    arrived = lax.all_to_all(outgoing, "vocab", split_axis=0, concat_axis=0, tiled=True)
+    arrived = lax.all_to_all(outgoing, ("vocab", "pair"), split_axis=0, concat_axis=0, tiled=True)
     row_sum = collect(arrived)
-    partial_sums = lax.all_to_all(row_sum, "rep", split_axis=0, concat_axis=0, tiled=True)
-    rep_index = lax.axis_index("rep").astype(jnp.int32).reshape(1)
+    partial_sums = lax.all_to_all(row_sum, REP, split_axis=0, concat_axis=0, tiled=True)
+    rep_index = lax.axis_index(REP).astype(jnp.int32).reshape(1)
     updated, rest, new_moment_one, new_moment_two = adam(
         rep_index, partial_sums, embed_table, norm_gain, moment_one, moment_two
     )
-    left = lax.all_gather(updated, "rep", axis=0, tiled=True)
-    right = lax.all_to_all(rest, "rep", split_axis=0, concat_axis=0, tiled=True)
+    left = lax.all_gather(updated, REP, axis=0, tiled=True)
+    right = lax.all_to_all(rest, REP, split_axis=0, concat_axis=0, tiled=True)
     new_table = jnp.concatenate([left, right], axis=1)
     return (new_table, new_moment_one, new_moment_two)
 
 
 def solution(mesh):
+    vocab, rep = mesh.devices.shape
+    paired = Mesh(mesh.devices.reshape(vocab, rep // 2, 2), ALL)
     placed = (
-        P(("vocab", "rep")),
-        P(("vocab", "rep"), None),
+        P(ALL),
+        P(ALL, None),
         P("vocab", None),
         P(),
-        P(("vocab", "rep"), None),
-        P(("vocab", "rep"), None),
+        P(ALL, None),
+        P(ALL, None),
     )
     return jax.shard_map(
         on_device,
-        mesh=mesh,
+        mesh=paired,
         in_specs=placed,
-        out_specs=(P("vocab", None), P(("vocab", "rep"), None), P(("vocab", "rep"), None)),
+        out_specs=(P("vocab", None), P(ALL, None), P(ALL, None)),
         check_vma=False,
     )

time: 155 us -> 148 us (0.955)
  waiting for transfers between devices: 32.1 us -> 20 us
  blocking collectives: 102 us -> 106 us
    all_to_all x2, waiting for transfers between devices: 32.1 us -> 20 us  [the longest x1 20 us: on_device(): lax.all_to_all(row_sum, REP, split_axis=0, concat_axis=0, tiled=True)]
    all_to_all x1, blocking collectives: 72.9 us -> 76.9 us  [on_device(): lax.all_to_all(outgoing, ('vocab', 'pair'), split_axis=0, concat_axis=0,...]
where the time goes in v3:
time: 148 us; the launch traced here: 146 us
  blocking collectives  106 us (72%)
  waiting for transfers between devices  20 us (14%)
  starting transfers between devices  9.7 us (7%)
  Pallas kernels  6.78 us (5%)
  local copies, waits for them, and re-layouts  1.95 us (1%)
    all_to_all x1, blocking collectives, on_device(): lax.all_to_all(outgoing, ('vocab', 'pair'), split_axis=0, concat_axis=0,...  76.9 us
    all_gather x1, blocking collectives, on_device(): left = lax.all_gather(updated, REP, axis=0, tiled=True)  29.3 us
    all_to_all x1, waiting for transfers between devices, on_device(): lax.all_to_all(row_sum, REP, split_axis=0, concat_axis=0, tiled=True)  20 us
    all_to_all x1, starting transfers between devices, on_device(): lax.all_to_all(row_sum, REP, split_axis=0, concat_axis=0, tiled=True)  6.31 us
    all_to_all x1, starting transfers between devices, on_device(): right = lax.all_to_all(rest, REP, split_axis=0, concat_axis=0, tiled=True)  3.38 us
  transfers between devices with their start and end apart: 2, of which 1 were waited for; matrix products, arithmetic and copies ran while one was open for 0% of the time, Pallas kernels for 0%

profile of v3, /device:TPU:6, one launch (start us, length us, event | category | flops | bytes accessed | tf_op | source)
XLA Modules:
  0.0 146.4 jit_solution(1961752804480599608)
XLA Ops:
  0.6 0.0 copy-start.3
  0.6 1.3 copy-done.3
  1.9 0.0 copy-start.4
  1.9 0.7 copy-done.4
  2.6 2.7 %pack.1 = bf16[1024,1280]{1,0:T(8,128)(2,1)S(1)} custom-call(s32[1,128]{1,0:T(1,128)S(1)} %bitcast.12, bf16[128,4608]{1,0:T(8,128)(2,1)S(1)} %copy-done.3), custom_call_target="tpu_custom_call" | custom-call | flops 1342177280 | bytes 3801088 | tf_op jit(solution)/shard_map/pack/pallas_call | solution.py:56
  5.2 76.9 %all_to_all.34 = bf16[128,8,1280]{2,1,0:T(8,128)(2,1)S(1)} all-to-all(bf16[128,8,1280]{2,1,0:T(8,128)(2,1)S(1)} %bitcast.10), channel_id=1, replica_groups=mesh['vocab'=64,'four'=4,'pair'=2] {'vocab','pair'}, dimensions={0} | all-to-all | bytes 5242880 | tf_op jit(solution)/shard_map/all_to_all | solution.py:188
  82.2 0.0 copy-start.5
  82.2 0.0 copy-start.1
  82.2 0.0 copy-start.2
  82.2 2.8 %collect.1 = bf16[128,2304]{1,0:T(8,128)(2,1)} custom-call(bf16[1024,1280]{1,0:T(8,128)(2,1)S(1)} %bitcast.8, bf16[1024,1280]{1,0:T(8,128)(2,1)S(1)} %bitcast.9), custom_call_target="tpu_custom_call" | custom-call | flops 603979776 | bytes 3211264 | tf_op jit(solution)/shard_map/collect/pallas_call | solution.py:94
  85.0 0.0 copy-start
  85.0 6.3 %all-to-all-start.1 = ((bf16[8,16,2304]{2,1,0:T(8,128)(2,1)}), bf16[8,16,2304]{2,1,0:T(8,128)(2,1)S(1)}, u32[]{:S(2)}, u32[]{:S(2)}) async-start(bf16[8,16,2304]{2,1,0:T(8,128)(2,1)} %bitcast.4), calls=%async_computation.1 | async-start | bytes 1179648 | tf_op jit(solution)/shard_map/all_to_all | solution.py:190
  91.3 0.0 copy-done.5
  91.3 20.0 %all-to-all-done.1 = bf16[8,16,2304]{2,1,0:T(8,128)(2,1)S(1)} async-done(((bf16[8,16,2304]{2,1,0:T(8,128)(2,1)}), bf16[8,16,2304]{2,1,0:T(8,128)(2,1)S(1)}, u32[]{:S(2)}, u32[]{:S(2)}) %all-to-all-start.1) | async-done | bytes 589856 | tf_op jit(solution)/shard_map/all_to_all | solution.py:190
  111.3 0.0 copy-done.1
  111.3 0.0 copy-done.2
  111.3 0.0 copy-done
  111.3 1.3 adam.1
  112.7 3.4 %all-to-all-start.2 = ((bf16[8,16,640]{2,1,0:T(8,128)(2,1)}), bf16[8,16,640]{2,1,0:T(8,128)(2,1)S(1)}, u32[]{:S(2)}, u32[]{:S(2)}) async-start(bf16[8,16,640]{2,1,0:T(8,128)(2,1)} %bitcast.6), calls=%async_computation.2 | async-start | bytes 327680 | tf_op jit(solution)/shard_map/all_to_all | solution.py:196
  116.1 29.3 %all_gather.3 = bf16[128,3968]{1,0:T(8,128)(2,1)S(1)} all-gather(bf16[16,3968]{1,0:T(8,128)(2,1)S(1)} %get-tuple-element.7), channel_id=1, replica_groups=mesh['vocab'=64,'four'=4,'pair'=2] {'four','pair'}, dimensions={0}, use_global_device_ids=true | all-gather | bytes 1142784 | tf_op jit(solution)/shard_map/all_gather | solution.py:195
  145.3 0.0 all-to-all-done.2
  145.3 1.1 pad_maximum_fusion
  (1 shorter events, 0.0 us)
Async XLA Ops:
  0.6 1.3 copy-start.3
  1.9 0.7 copy-start.4
  82.2 9.1 %copy-start.5 = (f32[4608]{0:T(1024)S(1)}, f32[4608]{0:T(1024)}, u32[]{:S(2)}) copy-start(f32[4608]{0:T(1024)} %param.9) | copy-start | bytes 55300
  82.2 29.1 %copy-start.1 = (f32[16,4608]{1,0:T(8,128)S(1)}, f32[16,4608]{1,0:T(8,128)}, u32[]{:S(2)}) copy-start(f32[16,4608]{1,0:T(8,128)} %one_ref.1) | copy-start | bytes 884740
  82.2 29.1 %copy-start.2 = (f32[16,4608]{1,0:T(8,128)S(1)}, f32[16,4608]{1,0:T(8,128)}, u32[]{:S(2)}) copy-start(f32[16,4608]{1,0:T(8,128)} %two_ref.1) | copy-start | bytes 884740
  85.0 26.4 %copy-start = (bf16[128,4608]{1,0:T(8,128)(2,1)S(1)}, bf16[128,4608]{1,0:T(8,128)(2,1)}, u32[]{:S(2)}) copy-start(bf16[128,4608]{1,0:T(8,128)(2,1)} %table_ref.1) | copy-start | bytes 3538948
  85.0 26.4 %all-to-all-start.1 = ((bf16[8,16,2304]{2,1,0:T(8,128)(2,1)}), bf16[8,16,2304]{2,1,0:T(8,128)(2,1)S(1)}, u32[]{:S(2)}, u32[]{:S(2)}) async-start(bf16[8,16,2304]{2,1,0:T(8,128)(2,1)} %bitcast.4), calls=%async_computation.1 | async-start | bytes 1179648 | tf_op jit(solution)/shard_map/all_to_all | solution.py:190
  112.7 32.7 %all-to-all-start.2 = ((bf16[8,16,640]{2,1,0:T(8,128)(2,1)}), bf16[8,16,640]{2,1,0:T(8,128)(2,1)S(1)}, u32[]{:S(2)}, u32[]{:S(2)}) async-start(bf16[8,16,640]{2,1,0:T(8,128)(2,1)} %bitcast.6), calls=%async_computation.2 | async-start | bytes 327680 | tf_op jit(solution)/shard_map/all_to_all | solution.py:196

commit v4 on v3

v4 whole, which is shorter than its diff:
```python
import math

import jax
import jax.numpy as jnp
from jax import lax
from jax.experimental import pallas as pl
from jax.experimental.pallas import tpu as pltpu
from jax.sharding import Mesh
from jax.sharding import PartitionSpec as P

beta_one = 0.9
beta_two = 0.95
learn_rate = 0.01
decay_rate = 0.01
adam_eps = 1e-08
norm_eps = 1e-06
correct_one = 0.9999734386011124
correct_two = 0.9940794707920236

SLOTS = 4
LANES = 128
GATHERED = 3968
MEMBERS = 4
HIGH = 8
LOW = 16
CODE = 64


def pack_body(ids_ref, cot_hbm, out_ref, cot_ref, piece_ref, slot_ref, sem):
    tok_count, width = cot_ref.shape
    piece = width // (2 * MEMBERS)
    lanes = out_ref.shape[-1]

    @pl.when(pl.program_id(0) == 0)
    def _():
        copy = pltpu.make_async_copy(cot_hbm, cot_ref, sem)
        copy.start()
        ids_along = jnp.broadcast_to(ids_ref[...], (tok_count, tok_count))
        ids_down = ids_along.T
        down = lax.broadcasted_iota(jnp.int32, (tok_count, tok_count), 0)
        along = lax.broadcasted_iota(jnp.int32, (tok_count, tok_count), 1)
        earlier = ((ids_along >> 7) == (ids_down >> 7)) & (down < along)
        position = jnp.sum(earlier.astype(jnp.int32), axis=0, keepdims=True)
        slot_ref[...] = (ids_ref[...] >> 7) * (2 * SLOTS) + position
        high = (ids_down >> 4) & (HIGH - 1)
        low = (ids_down & (LOW - 1)) + HIGH
        marks = ((along == high) | (along == low)).astype(jnp.bfloat16)[:, : lanes - piece]
        copy.wait()
        for at in range(2 * MEMBERS):
            member, half = at // 2, at % 2
            rows = slice(half * tok_count, (half + 1) * tok_count)
            piece_ref[member, rows, :piece] = cot_ref[:, at * piece : (at + 1) * piece]
            piece_ref[member, rows, piece:] = marks

    owners = out_ref.shape[0]
    block_rows = owners * 2 * SLOTS
    slots = jnp.concatenate([slot_ref[...], slot_ref[...] + SLOTS], axis=1)
    rows = lax.broadcasted_iota(jnp.int32, (block_rows, 2 * tok_count), 0)
    rows = rows + pl.program_id(0) * block_rows
    picks = (rows == slots).astype(jnp.bfloat16)
    for member in range(MEMBERS):
        moved = jnp.dot(picks, piece_ref[member], preferred_element_type=jnp.float32)
        out_ref[:, member] = moved.reshape(owners, 2 * SLOTS, lanes).astype(jnp.bfloat16)


def pack(token_ids, cotangent, peer_count):
    tok_count, width = cotangent.shape
    lanes = width // (2 * MEMBERS) + CODE
    steps = 4
    return pl.pallas_call(
        pack_body,
        grid=(steps,),
        in_specs=[
            pl.BlockSpec((1, tok_count), lambda i: (0, 0)),
            pl.BlockSpec(memory_space=pl.ANY),
        ],
        out_specs=pl.BlockSpec(
            (peer_count // steps, MEMBERS, 2 * SLOTS, lanes), lambda i: (i, 0, 0, 0)
        ),
        out_shape=jax.ShapeDtypeStruct((peer_count, MEMBERS, 2 * SLOTS, lanes), jnp.bfloat16),
        scratch_shapes=[
            pltpu.VMEM((tok_count, width), jnp.bfloat16),
            pltpu.VMEM((MEMBERS, 2 * tok_count, lanes), jnp.bfloat16),
            pltpu.VMEM((1, tok_count), jnp.int32),
            pltpu.SemaphoreType.DMA,
        ],
        compiler_params=pltpu.CompilerParams(vmem_limit_bytes=40 * 1024 * 1024),
        cost_estimate=pl.CostEstimate(
            flops=2 * peer_count * 2 * SLOTS * 2 * tok_count * MEMBERS * lanes,
            bytes_accessed=2 * (tok_count * width + peer_count * MEMBERS * 2 * SLOTS * lanes),
            transcendentals=0,
        ),
        name="pack",
    )(token_ids.reshape(1, tok_count), cotangent)


def collect_body(part_ref, out_ref, sum_ref):
    count, lanes = part_ref.shape
    piece = out_ref.shape[1] // 2
    step = pl.program_id(0)
    shard_row = lax.broadcasted_iota(jnp.int32, (LANES, CODE), 0)
    lane = lax.broadcasted_iota(jnp.int32, (LANES, CODE), 1)
    high = (lane == (shard_row >> 4)).astype(jnp.bfloat16)
    low = (lane == (shard_row & (LOW - 1)) + HIGH).astype(jnp.bfloat16)
    digits = jnp.concatenate([high, low], axis=0)
    found = lax.dot_general(
        digits,
        part_ref[:, piece:],
        (((1,), (1,)), ((), ())),
        preferred_element_type=jnp.float32,
    )
    picks = found[:LANES] * found[LANES:]
    half = lax.broadcasted_iota(jnp.int32, picks.shape, 1) & SLOTS
    picks = jnp.concatenate(
        [jnp.where(half == 0, picks, 0.0), jnp.where(half == 0, 0.0, picks)], axis=0
    ).astype(jnp.bfloat16)
    sums = jnp.dot(picks, part_ref[...], preferred_element_type=jnp.float32)

    @pl.when(step == 0)
    def _():
        sum_ref[...] = sums

    @pl.when(step > 0)
    def _():
        sum_ref[...] += sums

    @pl.when(step == pl.num_programs(0) - 1)
    def _():
        out_ref[:, :piece] = sum_ref[:LANES, :piece].astype(jnp.bfloat16)
        out_ref[:, piece:] = sum_ref[LANES:, :piece].astype(jnp.bfloat16)


def collect(arrived):
    count, lanes = arrived.shape
    piece = lanes - CODE
    steps = 4
    return pl.pallas_call(
        collect_body,
        grid=(steps,),
        in_specs=[pl.BlockSpec((count // steps, lanes), lambda i: (i, 0))],
        out_specs=pl.BlockSpec((LANES, 2 * piece), lambda i: (0, 0)),
        out_shape=jax.ShapeDtypeStruct((LANES, 2 * piece), jnp.bfloat16),
        scratch_shapes=[pltpu.VMEM((2 * LANES, lanes), jnp.float32)],
        compiler_params=pltpu.CompilerParams(vmem_limit_bytes=40 * 1024 * 1024),
        cost_estimate=pl.CostEstimate(
            flops=2 * count * 2 * LANES * lanes,
            bytes_accessed=2 * (count * lanes + 2 * LANES * piece),
            transcendentals=0,
        ),
        name="collect",
    )(arrived)


def adam_body(rep_ref, sum_ref, table_ref, gain_ref, one_ref, two_ref, up_ref, rest_ref, one_out, two_out):
    width = table_ref.shape[1]
    root = math.sqrt(width)
    params = table_ref[...].astype(jnp.float32)
    scaled = params * root
    rows = table_ref.shape[0]
    totals = []
    for member in range(MEMBERS):
        total = sum_ref[member * rows : (member + 1) * rows, :].astype(jnp.float32)
        for peer in range(member + MEMBERS, sum_ref.shape[0] // rows, MEMBERS):
            total = total + sum_ref[peer * rows : (peer + 1) * rows, :].astype(jnp.float32)
        totals.append(total)
    weighted = jnp.concatenate(totals, axis=1) * gain_ref[...]
    mean_square = jnp.mean(scaled * scaled, axis=-1, keepdims=True)
    inverse = lax.rsqrt(mean_square + norm_eps)
    inner_mean = jnp.mean(scaled * weighted, axis=-1, keepdims=True)
    grad = root * inverse * (weighted - scaled * (inverse * inverse * inner_mean))
    new_one = beta_one * one_ref[...] + (1.0 - beta_one) * grad
    new_two = beta_two * two_ref[...] + (1.0 - beta_two) * grad * grad
    one_out[...] = new_one
    two_out[...] = new_two
    update = (
        new_one / correct_one / (jnp.sqrt(new_two / correct_two) + adam_eps) + decay_rate * params
    )
    updated = (params - learn_rate * update).astype(jnp.bfloat16)
    up_ref[...] = updated[:, :GATHERED]
    rest = updated[:, GATHERED:]
    for peer in range(rest_ref.shape[0] // rows):
        rest_ref[peer * rows : (peer + 1) * rows, :] = rest


def adam(rep_index, partial_sums, embed_table, norm_gain, moment_one, moment_two):
    rows, width = moment_one.shape
    peers = embed_table.shape[0] // rows
    whole = pl.BlockSpec((rows, width), lambda i, rep: (0, 0))
    return pl.pallas_call(
        adam_body,
        grid_spec=pltpu.PrefetchScalarGridSpec(
            num_scalar_prefetch=1,
            grid=(1,),
            in_specs=[
                pl.BlockSpec((peers * rows, width // MEMBERS), lambda i, rep: (0, 0)),
                pl.BlockSpec((rows, width), lambda i, rep: (rep[0], 0)),
                pl.BlockSpec((1, width), lambda i, rep: (0, 0)),
                whole,
                whole,
            ],
            out_specs=[
                pl.BlockSpec((rows, GATHERED), lambda i, rep: (0, 0)),
                pl.BlockSpec((peers * rows, width - GATHERED), lambda i, rep: (0, 0)),
                whole,
                whole,
            ],
        ),
        out_shape=[
            jax.ShapeDtypeStruct((rows, GATHERED), jnp.bfloat16),
            jax.ShapeDtypeStruct((peers * rows, width - GATHERED), jnp.bfloat16),
            jax.ShapeDtypeStruct((rows, width), jnp.float32),
            jax.ShapeDtypeStruct((rows, width), jnp.float32),
        ],
        compiler_params=pltpu.CompilerParams(vmem_limit_bytes=40 * 1024 * 1024),
        cost_estimate=pl.CostEstimate(
            flops=40 * rows * width, bytes_accessed=24 * rows * width, transcendentals=rows * width
        ),
        name="adam",
    )(rep_index, partial_sums, embed_table, norm_gain.reshape(1, width), moment_one, moment_two)


REP = ("two", "four")
ALL = ("vocab", "two", "four")


def on_device(token_ids, cotangent, embed_table, norm_gain, moment_one, moment_two):
    peer_count = lax.axis_size("vocab")
    outgoing = pack(token_ids, cotangent, peer_count)
    outgoing = outgoing.reshape(-1, outgoing.shape[-1])
    arrived = lax.all_to_all(outgoing, ("vocab", "four"), split_axis=0, concat_axis=0, tiled=True)
    row_sum = collect(arrived)
    partial_sums = lax.all_to_all(row_sum, REP, split_axis=0, concat_axis=0, tiled=True)
    rep_index = lax.axis_index(REP).astype(jnp.int32).reshape(1)
    updated, rest, new_moment_one, new_moment_two = adam(
        rep_index, partial_sums, embed_table, norm_gain, moment_one, moment_two
    )
    left = lax.all_gather(updated, REP, axis=0, tiled=True)
    right = lax.all_to_all(rest, REP, split_axis=0, concat_axis=0, tiled=True)
    new_table = jnp.concatenate([left, right], axis=1)
    return (new_table, new_moment_one, new_moment_two)


def solution(mesh):
    vocab, rep = mesh.devices.shape
    fours = Mesh(mesh.devices.reshape(vocab, rep // MEMBERS, MEMBERS), ALL)
    placed = (
        P(ALL),
        P(ALL, None),
        P("vocab", None),
        P(),
        P(ALL, None),
        P(ALL, None),
    )
    return jax.shard_map(
        on_device,
        mesh=fours,
        in_specs=placed,
        out_specs=(P("vocab", None), P(ALL, None), P(ALL, None)),
        check_vma=False,
    )
```

time: 148 us -> 144 us (0.973)
  waiting for transfers between devices: 20 us -> 12 us
  blocking collectives: 106 us -> 111 us
  starting transfers between devices: 9.7 us -> 7.8 us
    all_to_all x1, waiting for transfers between devices: 20 us -> 12 us  [on_device(): lax.all_to_all(row_sum, REP, split_axis=0, concat_axis=0, tiled=True)]
    all_to_all x1, blocking collectives: 76.9 us -> 82.8 us  [on_device(): lax.all_to_all(outgoing, ('vocab', 'four'), split_axis=0, concat_axis=0,...]
    all_to_all x1, starting transfers between devices: 6.31 us -> 4.42 us  [on_device(): lax.all_to_all(row_sum, REP, split_axis=0, concat_axis=0, tiled=True)]
where the time goes in v4:
time: 144 us; the launch traced here: 142 us
  blocking collectives  111 us (77%)
  waiting for transfers between devices  12 us (8%)
  starting transfers between devices  7.8 us (5%)
  Pallas kernels  7.06 us (5%)
  local copies, waits for them, and re-layouts  1.95 us (1%)
    all_to_all x1, blocking collectives, on_device(): lax.all_to_all(outgoing, ('vocab', 'four'), split_axis=0, concat_axis=0,...  82.8 us
    all_gather x1, blocking collectives, on_device(): left = lax.all_gather(updated, REP, axis=0, tiled=True)  28.5 us
    all_to_all x1, waiting for transfers between devices, on_device(): lax.all_to_all(row_sum, REP, split_axis=0, concat_axis=0, tiled=True)  12 us
    all_to_all x1, starting transfers between devices, on_device(): lax.all_to_all(row_sum, REP, split_axis=0, concat_axis=0, tiled=True)  4.42 us
    pallas_call x1, Pallas kernels, collect(): pl.pallas_call(collect_body, grid=(steps,), in_specs=[pl.BlockSpec((count...  3.56 us
    all_to_all x1, starting transfers between devices, on_device(): right = lax.all_to_all(rest, REP, split_axis=0, concat_axis=0, tiled=True)  3.38 us
  transfers between devices with their start and end apart: 2, of which 1 were waited for; matrix products, arithmetic and copies ran while one was open for 0% of the time, Pallas kernels for 0%

profile of v4, /device:TPU:6, one launch (start us, length us, event | category | flops | bytes accessed | tf_op | source)
XLA Modules:
  0.0 142.0 jit_solution(8456172071497318508)
XLA Ops:
  0.6 0.0 copy-start.1
  0.6 1.3 copy-done.1
  1.9 0.0 copy-start.4
  1.9 0.7 copy-done.4
  2.6 2.2 %pack.1 = bf16[64,4,8,640]{3,2,1,0:T(8,128)(2,1)S(1)} custom-call(s32[1,128]{1,0:T(1,128)S(1)} %bitcast.11, bf16[128,4608]{1,0:T(8,128)(2,1)S(1)} %copy-done.1), custom_call_target="tpu_custom_call" | custom-call | flops 671088640 | bytes 3801088 | tf_op jit(solution)/shard_map/pack/pallas_call | solution.py:70
  4.8 82.8 %all_to_all.34 = bf16[256,8,640]{2,1,0:T(8,128)(2,1)S(1)} all-to-all(bf16[256,8,640]{2,1,0:T(8,128)(2,1)S(1)} %bitcast.9), channel_id=1, replica_groups=mesh['vocab'=64,'two'=2,'four'=4] {'vocab','four'}, dimensions={0} | all-to-all | bytes 5242880 | tf_op jit(solution)/shard_map/all_to_all | solution.py:230
  87.6 0.0 copy-start.5
  87.6 0.0 copy-start
  87.6 0.0 copy-start.2
  87.6 0.0 copy-start.3
  87.6 3.6 %collect.1 = bf16[128,1152]{1,0:T(8,128)(2,1)} custom-call(bf16[2048,640]{1,0:T(8,128)(2,1)S(1)} %bitcast.8), custom_call_target="tpu_custom_call" | custom-call | flops 671088640 | bytes 2916352 | tf_op jit(solution)/shard_map/collect/pallas_call | solution.py:137
  91.2 4.4 %all-to-all-start.1 = ((bf16[8,16,1152]{2,1,0:T(8,128)(2,1)}), bf16[8,16,1152]{2,1,0:T(8,128)(2,1)S(1)}, u32[]{:S(2)}, u32[]{:S(2)}) async-start(bf16[8,16,1152]{2,1,0:T(8,128)(2,1)} %bitcast.4), calls=%async_computation.1 | async-start | bytes 589824 | tf_op jit(solution)/shard_map/all_to_all | solution.py:232
  95.6 0.0 copy-done.5
  95.6 12.0 %all-to-all-done.1 = bf16[8,16,1152]{2,1,0:T(8,128)(2,1)S(1)} async-done(((bf16[8,16,1152]{2,1,0:T(8,128)(2,1)}), bf16[8,16,1152]{2,1,0:T(8,128)(2,1)S(1)}, u32[]{:S(2)}, u32[]{:S(2)}) %all-to-all-start.1) | async-done | bytes 294944 | tf_op jit(solution)/shard_map/all_to_all | solution.py:232
  107.6 0.0 copy-done
  107.6 0.0 copy-done.2
  107.7 0.0 copy-done.3
  107.7 1.3 adam.1
  109.0 3.4 %all-to-all-start.2 = ((bf16[8,16,640]{2,1,0:T(8,128)(2,1)}), bf16[8,16,640]{2,1,0:T(8,128)(2,1)S(1)}, u32[]{:S(2)}, u32[]{:S(2)}) async-start(bf16[8,16,640]{2,1,0:T(8,128)(2,1)} %bitcast.6), calls=%async_computation.2 | async-start | bytes 327680 | tf_op jit(solution)/shard_map/all_to_all | solution.py:238
  112.4 28.5 %all_gather.3 = bf16[128,3968]{1,0:T(8,128)(2,1)S(1)} all-gather(bf16[16,3968]{1,0:T(8,128)(2,1)S(1)} %get-tuple-element.7), channel_id=1, replica_groups=mesh['vocab'=64,'two'=2,'four'=4] {'two','four'}, dimensions={0}, use_global_device_ids=true | all-gather | bytes 1142784 | tf_op jit(solution)/shard_map/all_gather | solution.py:237
  140.9 0.0 all-to-all-done.2
  140.9 1.1 pad_maximum_fusion
  (1 shorter events, 0.0 us)
Async XLA Ops:
  0.6 1.3 copy-start.1
  1.9 0.7 copy-start.4
  87.6 8.0 %copy-start.5 = (f32[4608]{0:T(1024)S(1)}, f32[4608]{0:T(1024)}, u32[]{:S(2)}) copy-start(f32[4608]{0:T(1024)} %param.9) | copy-start | bytes 55300
  87.6 20.0 %copy-start = (bf16[128,4608]{1,0:T(8,128)(2,1)S(1)}, bf16[128,4608]{1,0:T(8,128)(2,1)}, u32[]{:S(2)}) copy-start(bf16[128,4608]{1,0:T(8,128)(2,1)} %table_ref.1) | copy-start | bytes 3538948
  87.6 20.0 %copy-start.2 = (f32[16,4608]{1,0:T(8,128)S(1)}, f32[16,4608]{1,0:T(8,128)}, u32[]{:S(2)}) copy-start(f32[16,4608]{1,0:T(8,128)} %one_ref.1) | copy-start | bytes 884740
  87.6 20.0 %copy-start.3 = (f32[16,4608]{1,0:T(8,128)S(1)}, f32[16,4608]{1,0:T(8,128)}, u32[]{:S(2)}) copy-start(f32[16,4608]{1,0:T(8,128)} %two_ref.1) | copy-start | bytes 884740
  91.2 16.5 %all-to-all-start.1 = ((bf16[8,16,1152]{2,1,0:T(8,128)(2,1)}), bf16[8,16,1152]{2,1,0:T(8,128)(2,1)S(1)}, u32[]{:S(2)}, u32[]{:S(2)}) async-start(bf16[8,16,1152]{2,1,0:T(8,128)(2,1)} %bitcast.4), calls=%async_computation.1 | async-start | bytes 589824 | tf_op jit(solution)/shard_map/all_to_all | solution.py:232
  109.0 31.9 %all-to-all-start.2 = ((bf16[8,16,640]{2,1,0:T(8,128)(2,1)}), bf16[8,16,640]{2,1,0:T(8,128)(2,1)S(1)}, u32[]{:S(2)}, u32[]{:S(2)}) async-start(bf16[8,16,640]{2,1,0:T(8,128)(2,1)} %bitcast.6), calls=%async_computation.2 | async-start | bytes 327680 | tf_op jit(solution)/shard_map/all_to_all | solution.py:238

commit v5 on v4

--- a/solution.py
+++ b/solution.py
@@ -24,17 +24,21 @@
 HIGH = 8
 LOW = 16
 CODE = 64
-
-
-def pack_body(ids_ref, cot_hbm, out_ref, cot_ref, piece_ref, slot_ref, sem):
+PACK_VMEM = 60 * 1024 * 1024
+
+
+def pack_body(ids_hbm, cot_hbm, out_ref, ids_ref, cot_ref, piece_ref, slot_ref, sems):
     tok_count, width = cot_ref.shape
     piece = width // (2 * MEMBERS)
     lanes = out_ref.shape[-1]
 
     @pl.when(pl.program_id(0) == 0)
     def _():
-        copy = pltpu.make_async_copy(cot_hbm, cot_ref, sem)
-        copy.start()
+        copy_ids = pltpu.make_async_copy(ids_hbm, ids_ref, sems.at[0])
+        copy_cot = pltpu.make_async_copy(cot_hbm, cot_ref, sems.at[1])
+        copy_ids.start()
+        copy_cot.start()
+        copy_ids.wait()
         ids_along = jnp.broadcast_to(ids_ref[...], (tok_count, tok_count))
         ids_down = ids_along.T
         down = lax.broadcasted_iota(jnp.int32, (tok_count, tok_count), 0)
@@ -43,14 +47,17 @@
         position = jnp.sum(earlier.astype(jnp.int32), axis=0, keepdims=True)
         slot_ref[...] = (ids_ref[...] >> 7) * (2 * SLOTS) + position
         high = (ids_down >> 4) & (HIGH - 1)
-        low = (ids_down & (LOW - 1)) + HIGH
-        marks = ((along == high) | (along == low)).astype(jnp.bfloat16)[:, : lanes - piece]
-        copy.wait()
+        low = (ids_down & (LOW - 1)) + 2 * HIGH
+        marks = [
+            ((along == high + half * HIGH) | (along == low)).astype(jnp.bfloat16)[:, : lanes - piece]
+            for half in range(2)
+        ]
+        copy_cot.wait()
         for at in range(2 * MEMBERS):
             member, half = at // 2, at % 2
             rows = slice(half * tok_count, (half + 1) * tok_count)
             piece_ref[member, rows, :piece] = cot_ref[:, at * piece : (at + 1) * piece]
-            piece_ref[member, rows, piece:] = marks
+            piece_ref[member, rows, piece:] = marks[half]
 
     owners = out_ref.shape[0]
     block_rows = owners * 2 * SLOTS
@@ -70,21 +77,19 @@
     return pl.pallas_call(
         pack_body,
         grid=(steps,),
-        in_specs=[
-            pl.BlockSpec((1, tok_count), lambda i: (0, 0)),
-            pl.BlockSpec(memory_space=pl.ANY),
-        ],
+        in_specs=[pl.BlockSpec(memory_space=pl.ANY), pl.BlockSpec(memory_space=pl.ANY)],
         out_specs=pl.BlockSpec(
             (peer_count // steps, MEMBERS, 2 * SLOTS, lanes), lambda i: (i, 0, 0, 0)
         ),
         out_shape=jax.ShapeDtypeStruct((peer_count, MEMBERS, 2 * SLOTS, lanes), jnp.bfloat16),
         scratch_shapes=[
+            pltpu.VMEM((1, tok_count), jnp.int32),
             pltpu.VMEM((tok_count, width), jnp.bfloat16),
             pltpu.VMEM((MEMBERS, 2 * tok_count, lanes), jnp.bfloat16),
             pltpu.VMEM((1, tok_count), jnp.int32),
-            pltpu.SemaphoreType.DMA,
+            pltpu.SemaphoreType.DMA((2,)),
         ],
-        compiler_params=pltpu.CompilerParams(vmem_limit_bytes=40 * 1024 * 1024),
+        compiler_params=pltpu.CompilerParams(vmem_limit_bytes=PACK_VMEM),
         cost_estimate=pl.CostEstimate(
             flops=2 * peer_count * 2 * SLOTS * 2 * tok_count * MEMBERS * lanes,
             bytes_accessed=2 * (tok_count * width + peer_count * MEMBERS * 2 * SLOTS * lanes),
@@ -94,53 +99,39 @@
     )(token_ids.reshape(1, tok_count), cotangent)
 
 
-def collect_body(part_ref, out_ref, sum_ref):
-    count, lanes = part_ref.shape
+def collect_body(part_ref, out_ref):
     piece = out_ref.shape[1] // 2
-    step = pl.program_id(0)
     shard_row = lax.broadcasted_iota(jnp.int32, (LANES, CODE), 0)
     lane = lax.broadcasted_iota(jnp.int32, (LANES, CODE), 1)
-    high = (lane == (shard_row >> 4)).astype(jnp.bfloat16)
-    low = (lane == (shard_row & (LOW - 1)) + HIGH).astype(jnp.bfloat16)
-    digits = jnp.concatenate([high, low], axis=0)
+    high = shard_row >> 4
+    low = (shard_row & (LOW - 1)) + 2 * HIGH
+    digits = jnp.concatenate(
+        [(lane == value).astype(jnp.bfloat16) for value in (high, high + HIGH, low)], axis=0
+    )
     found = lax.dot_general(
         digits,
         part_ref[:, piece:],
         (((1,), (1,)), ((), ())),
         preferred_element_type=jnp.float32,
     )
-    picks = found[:LANES] * found[LANES:]
-    half = lax.broadcasted_iota(jnp.int32, picks.shape, 1) & SLOTS
-    picks = jnp.concatenate(
-        [jnp.where(half == 0, picks, 0.0), jnp.where(half == 0, 0.0, picks)], axis=0
+    picks = (found[: 2 * LANES].reshape(2, LANES, -1) * found[2 * LANES :][None]).reshape(
+        2 * LANES, -1
+    )
+    sums = jnp.dot(
+        picks.astype(jnp.bfloat16), part_ref[...], preferred_element_type=jnp.float32
     ).astype(jnp.bfloat16)
-    sums = jnp.dot(picks, part_ref[...], preferred_element_type=jnp.float32)
-
-    @pl.when(step == 0)
-    def _():
-        sum_ref[...] = sums
-
-    @pl.when(step > 0)
-    def _():
-        sum_ref[...] += sums
-
-    @pl.when(step == pl.num_programs(0) - 1)
-    def _():
-        out_ref[:, :piece] = sum_ref[:LANES, :piece].astype(jnp.bfloat16)
-        out_ref[:, piece:] = sum_ref[LANES:, :piece].astype(jnp.bfloat16)
+    out_ref[:, :piece] = sums[:LANES, :piece]
+    out_ref[:, piece:] = sums[LANES:, :piece]
 
 
 def collect(arrived):
     count, lanes = arrived.shape
     piece = lanes - CODE
-    steps = 4
     return pl.pallas_call(
         collect_body,
-        grid=(steps,),
-        in_specs=[pl.BlockSpec((count // steps, lanes), lambda i: (i, 0))],
-        out_specs=pl.BlockSpec((LANES, 2 * piece), lambda i: (0, 0)),
+        in_specs=[pl.BlockSpec(memory_space=pltpu.VMEM)],
+        out_specs=pl.BlockSpec(memory_space=pltpu.VMEM),
         out_shape=jax.ShapeDtypeStruct((LANES, 2 * piece), jnp.bfloat16),
-        scratch_shapes=[pltpu.VMEM((2 * LANES, lanes), jnp.float32)],
         compiler_params=pltpu.CompilerParams(vmem_limit_bytes=40 * 1024 * 1024),
         cost_estimate=pl.CostEstimate(
             flops=2 * count * 2 * LANES * lanes,

time: 144 us -> 143 us (level)
  local copies, waits for them, and re-layouts: 1.95 us -> 0.03 us
    unnamed x12 -> x8, local copies, waits for them, and re-layouts: 1.93 us -> 0.01 us
where the time goes in v5:
time: 143 us; the launch traced here: 141 us
  blocking collectives  112 us (78%)
  waiting for transfers between devices  12 us (8%)
  Pallas kernels  8.03 us (6%)
  starting transfers between devices  7.81 us (5%)
    all_to_all x1, blocking collectives, on_device(): lax.all_to_all(outgoing, ('vocab', 'four'), split_axis=0, concat_axis=0,...  83.1 us
    all_gather x1, blocking collectives, on_device(): left = lax.all_gather(updated, REP, axis=0, tiled=True)  28.5 us
    all_to_all x1, waiting for transfers between devices, on_device(): lax.all_to_all(row_sum, REP, split_axis=0, concat_axis=0, tiled=True)  12 us
    pallas_call x1, Pallas kernels, pack(): pl.pallas_call(pack_body, grid=(steps,), in_specs=[pl.BlockSpec(memory_sp...  4.48 us
    all_to_all x1, starting transfers between devices, on_device(): lax.all_to_all(row_sum, REP, split_axis=0, concat_axis=0, tiled=True)  4.43 us
    all_to_all x1, starting transfers between devices, on_device(): right = lax.all_to_all(rest, REP, split_axis=0, concat_axis=0, tiled=True)  3.38 us
  transfers between devices with their start and end apart: 2, of which 1 were waited for; matrix products, arithmetic and copies ran while one was open for 0% of the time, Pallas kernels for 0%

profile of v5, /device:TPU:6, one launch (start us, length us, event | category | flops | bytes accessed | tf_op | source)
XLA Modules:
  0.0 141.3 jit_solution(8027396511491701909)
XLA Ops:
  0.6 4.5 %pack.1 = bf16[64,4,8,640]{3,2,1,0:T(8,128)(2,1)} custom-call(s32[1,128]{1,0:T(1,128)} %bitcast.12, bf16[128,4608]{1,0:T(8,128)(2,1)} %cot_hbm.1), custom_call_target="tpu_custom_call" | custom-call | flops 671088640 | bytes 3801088 | tf_op jit(solution)/shard_map/pack/pallas_call | solution.py:77
  5.1 83.1 %all_to_all.34 = bf16[256,8,640]{2,1,0:T(8,128)(2,1)S(1)} all-to-all(bf16[256,8,640]{2,1,0:T(8,128)(2,1)} %bitcast.10), channel_id=1, replica_groups=mesh['vocab'=64,'two'=2,'four'=4] {'vocab','four'}, dimensions={0} | all-to-all | bytes 5242880 | tf_op jit(solution)/shard_map/all_to_all | solution.py:221
  88.2 0.0 copy-start.3
  88.2 0.0 copy-start
  88.2 0.0 copy-start.1
  88.2 0.0 copy-start.2
  88.2 2.3 %collect.1 = bf16[128,1152]{1,0:T(8,128)(2,1)} custom-call(bf16[2048,640]{1,0:T(8,128)(2,1)S(1)} %bitcast.8), custom_call_target="tpu_custom_call" | custom-call | flops 671088640 | bytes 2916352 | tf_op jit(solution)/shard_map/collect/pallas_call | solution.py:130
  90.4 4.4 %all-to-all-start.1 = ((bf16[8,16,1152]{2,1,0:T(8,128)(2,1)}), bf16[8,16,1152]{2,1,0:T(8,128)(2,1)S(1)}, u32[]{:S(2)}, u32[]{:S(2)}) async-start(bf16[8,16,1152]{2,1,0:T(8,128)(2,1)} %bitcast.4), calls=%async_computation.1 | async-start | bytes 589824 | tf_op jit(solution)/shard_map/all_to_all | solution.py:223
  94.9 0.0 copy-done.3
  94.9 12.0 %all-to-all-done.1 = bf16[8,16,1152]{2,1,0:T(8,128)(2,1)S(1)} async-done(((bf16[8,16,1152]{2,1,0:T(8,128)(2,1)}), bf16[8,16,1152]{2,1,0:T(8,128)(2,1)S(1)}, u32[]{:S(2)}, u32[]{:S(2)}) %all-to-all-start.1) | async-done | bytes 294944 | tf_op jit(solution)/shard_map/all_to_all | solution.py:223
  106.9 0.0 copy-done
  106.9 0.0 copy-done.1
  106.9 0.0 copy-done.2
  106.9 1.3 adam.1
  108.2 3.4 %all-to-all-start.2 = ((bf16[8,16,640]{2,1,0:T(8,128)(2,1)}), bf16[8,16,640]{2,1,0:T(8,128)(2,1)S(1)}, u32[]{:S(2)}, u32[]{:S(2)}) async-start(bf16[8,16,640]{2,1,0:T(8,128)(2,1)} %bitcast.6), calls=%async_computation.2 | async-start | bytes 327680 | tf_op jit(solution)/shard_map/all_to_all | solution.py:229
  111.6 28.5 %all_gather.3 = bf16[128,3968]{1,0:T(8,128)(2,1)S(1)} all-gather(bf16[16,3968]{1,0:T(8,128)(2,1)S(1)} %get-tuple-element.7), channel_id=1, replica_groups=mesh['vocab'=64,'two'=2,'four'=4] {'two','four'}, dimensions={0}, use_global_device_ids=true | all-gather | bytes 1142784 | tf_op jit(solution)/shard_map/all_gather | solution.py:228
  140.2 0.0 all-to-all-done.2
  140.2 1.1 pad_maximum_fusion
  (1 shorter events, 0.0 us)
Async XLA Ops:
  88.2 6.7 %copy-start.3 = (f32[4608]{0:T(1024)S(1)}, f32[4608]{0:T(1024)}, u32[]{:S(2)}) copy-start(f32[4608]{0:T(1024)} %param.9) | copy-start | bytes 55300
  88.2 18.8 %copy-start = (bf16[128,4608]{1,0:T(8,128)(2,1)S(1)}, bf16[128,4608]{1,0:T(8,128)(2,1)}, u32[]{:S(2)}) copy-start(bf16[128,4608]{1,0:T(8,128)(2,1)} %table_ref.1) | copy-start | bytes 3538948
  88.2 18.8 %copy-start.1 = (f32[16,4608]{1,0:T(8,128)S(1)}, f32[16,4608]{1,0:T(8,128)}, u32[]{:S(2)}) copy-start(f32[16,4608]{1,0:T(8,128)} %one_ref.1) | copy-start | bytes 884740
  88.2 18.8 %copy-start.2 = (f32[16,4608]{1,0:T(8,128)S(1)}, f32[16,4608]{1,0:T(8,128)}, u32[]{:S(2)}) copy-start(f32[16,4608]{1,0:T(8,128)} %two_ref.1) | copy-start | bytes 884740
  90.4 16.5 %all-to-all-start.1 = ((bf16[8,16,1152]{2,1,0:T(8,128)(2,1)}), bf16[8,16,1152]{2,1,0:T(8,128)(2,1)S(1)}, u32[]{:S(2)}, u32[]{:S(2)}) async-start(bf16[8,16,1152]{2,1,0:T(8,128)(2,1)} %bitcast.4), calls=%async_computation.1 | async-start | bytes 589824 | tf_op jit(solution)/shard_map/all_to_all | solution.py:223
  108.2 31.9 %all-to-all-start.2 = ((bf16[8,16,640]{2,1,0:T(8,128)(2,1)}), bf16[8,16,640]{2,1,0:T(8,128)(2,1)S(1)}, u32[]{:S(2)}, u32[]{:S(2)}) async-start(bf16[8,16,640]{2,1,0:T(8,128)(2,1)} %bitcast.6), calls=%async_computation.2 | async-start | bytes 327680 | tf_op jit(solution)/shard_map/all_to_all | solution.py:229

commit v6 on v5

--- a/solution.py
+++ b/solution.py
@@ -24,72 +24,80 @@
 HIGH = 8
 LOW = 16
 CODE = 64
-PACK_VMEM = 60 * 1024 * 1024
-
-
-def pack_body(ids_hbm, cot_hbm, out_ref, ids_ref, cot_ref, piece_ref, slot_ref, sems):
+
+
+def pack_body(ids_hbm, cot_hbm, out_hbm, ids_ref, cot_ref, piece_ref, out_ref, sems, out_sems):
     tok_count, width = cot_ref.shape
-    piece = width // (2 * MEMBERS)
-    lanes = out_ref.shape[-1]
-
-    @pl.when(pl.program_id(0) == 0)
-    def _():
-        copy_ids = pltpu.make_async_copy(ids_hbm, ids_ref, sems.at[0])
-        copy_cot = pltpu.make_async_copy(cot_hbm, cot_ref, sems.at[1])
-        copy_ids.start()
-        copy_cot.start()
-        copy_ids.wait()
-        ids_along = jnp.broadcast_to(ids_ref[...], (tok_count, tok_count))
-        ids_down = ids_along.T
-        down = lax.broadcasted_iota(jnp.int32, (tok_count, tok_count), 0)
-        along = lax.broadcasted_iota(jnp.int32, (tok_count, tok_count), 1)
-        earlier = ((ids_along >> 7) == (ids_down >> 7)) & (down < along)
-        position = jnp.sum(earlier.astype(jnp.int32), axis=0, keepdims=True)
-        slot_ref[...] = (ids_ref[...] >> 7) * (2 * SLOTS) + position
-        high = (ids_down >> 4) & (HIGH - 1)
-        low = (ids_down & (LOW - 1)) + 2 * HIGH
-        marks = [
-            ((along == high + half * HIGH) | (along == low)).astype(jnp.bfloat16)[:, : lanes - piece]
-            for half in range(2)
-        ]
-        copy_cot.wait()
-        for at in range(2 * MEMBERS):
-            member, half = at // 2, at % 2
-            rows = slice(half * tok_count, (half + 1) * tok_count)
-            piece_ref[member, rows, :piece] = cot_ref[:, at * piece : (at + 1) * piece]
-            piece_ref[member, rows, piece:] = marks[half]
-
-    owners = out_ref.shape[0]
-    block_rows = owners * 2 * SLOTS
-    slots = jnp.concatenate([slot_ref[...], slot_ref[...] + SLOTS], axis=1)
-    rows = lax.broadcasted_iota(jnp.int32, (block_rows, 2 * tok_count), 0)
-    rows = rows + pl.program_id(0) * block_rows
+    own = width // MEMBERS
+    piece = own // 2
+    _, owners, per_owner, lanes = out_ref.shape
+    copy_ids = pltpu.make_async_copy(ids_hbm, ids_ref, sems.at[MEMBERS])
+    copies = [
+        pltpu.make_async_copy(
+            cot_hbm.at[:, member * own : (member + 1) * own],
+            cot_ref.at[:, member * own : (member + 1) * own],
+            sems.at[member],
+        )
+        for member in range(MEMBERS)
+    ]
+    copy_ids.start()
+    for copy in copies:
+        copy.start()
+    copy_ids.wait()
+    ids_along = jnp.broadcast_to(ids_ref[...], (tok_count, tok_count))
+    ids_down = ids_along.T
+    down = lax.broadcasted_iota(jnp.int32, (tok_count, tok_count), 0)
+    along = lax.broadcasted_iota(jnp.int32, (tok_count, tok_count), 1)
+    earlier = ((ids_along >> 7) == (ids_down >> 7)) & (down < along)
+    position = jnp.sum(earlier.astype(jnp.int32), axis=0, keepdims=True)
+    slot = (ids_ref[...] >> 7) * per_owner + position
+    slots = jnp.concatenate([slot, slot + SLOTS], axis=1)
+    rows = lax.broadcasted_iota(jnp.int32, (owners * per_owner, 2 * tok_count), 0)
     picks = (rows == slots).astype(jnp.bfloat16)
+    high = (ids_down >> 4) & (HIGH - 1)
+    low = (ids_down & (LOW - 1)) + 2 * HIGH
+    marks = [
+        ((along == high + half * HIGH) | (along == low)).astype(jnp.bfloat16)[:, : lanes - piece]
+        for half in range(2)
+    ]
     for member in range(MEMBERS):
+        for half in range(2):
+            piece_ref[member, half * tok_count : (half + 1) * tok_count, piece:] = marks[half]
+    sends = []
+    for member in range(MEMBERS):
+        copies[member].wait()
+        for half in range(2):
+            at = member * own + half * piece
+            piece_ref[member, half * tok_count : (half + 1) * tok_count, :piece] = cot_ref[
+                :, at : at + piece
+            ]
         moved = jnp.dot(picks, piece_ref[member], preferred_element_type=jnp.float32)
-        out_ref[:, member] = moved.reshape(owners, 2 * SLOTS, lanes).astype(jnp.bfloat16)
+        out_ref[member] = moved.reshape(owners, per_owner, lanes).astype(jnp.bfloat16)
+        sends.append(
+            pltpu.make_async_copy(out_ref.at[member], out_hbm.at[:, member], out_sems.at[member])
+        )
+        sends[member].start()
+    for send in sends:
+        send.wait()
 
 
 def pack(token_ids, cotangent, peer_count):
     tok_count, width = cotangent.shape
     lanes = width // (2 * MEMBERS) + CODE
-    steps = 4
     return pl.pallas_call(
         pack_body,
-        grid=(steps,),
         in_specs=[pl.BlockSpec(memory_space=pl.ANY), pl.BlockSpec(memory_space=pl.ANY)],
-        out_specs=pl.BlockSpec(
-            (peer_count // steps, MEMBERS, 2 * SLOTS, lanes), lambda i: (i, 0, 0, 0)
-        ),
+        out_specs=pl.BlockSpec(memory_space=pl.ANY),
         out_shape=jax.ShapeDtypeStruct((peer_count, MEMBERS, 2 * SLOTS, lanes), jnp.bfloat16),
         scratch_shapes=[
             pltpu.VMEM((1, tok_count), jnp.int32),
             pltpu.VMEM((tok_count, width), jnp.bfloat16),
             pltpu.VMEM((MEMBERS, 2 * tok_count, lanes), jnp.bfloat16),
-            pltpu.VMEM((1, tok_count), jnp.int32),
-            pltpu.SemaphoreType.DMA((2,)),
+            pltpu.VMEM((MEMBERS, peer_count, 2 * SLOTS, lanes), jnp.bfloat16),
+            pltpu.SemaphoreType.DMA((MEMBERS + 1,)),
+            pltpu.SemaphoreType.DMA((MEMBERS,)),
         ],
-        compiler_params=pltpu.CompilerParams(vmem_limit_bytes=PACK_VMEM),
+        compiler_params=pltpu.CompilerParams(vmem_limit_bytes=58 * 1024 * 1024),
         cost_estimate=pl.CostEstimate(
             flops=2 * peer_count * 2 * SLOTS * 2 * tok_count * MEMBERS * lanes,
             bytes_accessed=2 * (tok_count * width + peer_count * MEMBERS * 2 * SLOTS * lanes),

time: 143 us -> 143 us (level)
  no operation moved by 1% of the time
where the time goes in v6:
time: 143 us; the launch traced here: 141 us
  blocking collectives  112 us (78%)
  waiting for transfers between devices  12 us (8%)
  starting transfers between devices  7.8 us (5%)
  Pallas kernels  7.5 us (5%)
    all_to_all x1, blocking collectives, on_device(): lax.all_to_all(outgoing, ('vocab', 'four'), split_axis=0, concat_axis=0,...  83.1 us
    all_gather x1, blocking collectives, on_device(): left = lax.all_gather(updated, REP, axis=0, tiled=True)  28.5 us
    all_to_all x1, waiting for transfers between devices, on_device(): lax.all_to_all(row_sum, REP, split_axis=0, concat_axis=0, tiled=True)  12 us
    all_to_all x1, starting transfers between devices, on_device(): lax.all_to_all(row_sum, REP, split_axis=0, concat_axis=0, tiled=True)  4.42 us
    pallas_call x1, Pallas kernels, pack(): pl.pallas_call(pack_body, in_specs=[pl.BlockSpec(memory_space=pl.ANY), pl...  3.94 us
    all_to_all x1, starting transfers between devices, on_device(): right = lax.all_to_all(rest, REP, split_axis=0, concat_axis=0, tiled=True)  3.38 us
  transfers between devices with their start and end apart: 2, of which 1 were waited for; matrix products, arithmetic and copies ran while one was open for 0% of the time, Pallas kernels for 0%

profile of v6, /device:TPU:6, one launch (start us, length us, event | category | flops | bytes accessed | tf_op | source)
XLA Modules:
  0.0 140.7 jit_solution(8584909862674348546)
XLA Ops:
  0.6 3.9 %pack.1 = bf16[64,4,8,640]{3,2,1,0:T(8,128)(2,1)} custom-call(s32[1,128]{1,0:T(1,128)} %bitcast.12, bf16[128,4608]{1,0:T(8,128)(2,1)} %cot_hbm.1), custom_call_target="tpu_custom_call" | custom-call | flops 671088640 | bytes 3801088 | tf_op jit(solution)/shard_map/pack/pallas_call | solution.py:87
  4.6 83.1 %all_to_all.34 = bf16[256,8,640]{2,1,0:T(8,128)(2,1)S(1)} all-to-all(bf16[256,8,640]{2,1,0:T(8,128)(2,1)} %bitcast.10), channel_id=1, replica_groups=mesh['vocab'=64,'two'=2,'four'=4] {'vocab','four'}, dimensions={0} | all-to-all | bytes 5242880 | tf_op jit(solution)/shard_map/all_to_all | solution.py:229
  87.6 0.0 copy-start.3
  87.6 0.0 copy-start
  87.6 0.0 copy-start.1
  87.6 0.0 copy-start.2
  87.6 2.3 %collect.1 = bf16[128,1152]{1,0:T(8,128)(2,1)} custom-call(bf16[2048,640]{1,0:T(8,128)(2,1)S(1)} %bitcast.8), custom_call_target="tpu_custom_call" | custom-call | flops 671088640 | bytes 2916352 | tf_op jit(solution)/shard_map/collect/pallas_call | solution.py:138
  89.9 4.4 %all-to-all-start.1 = ((bf16[8,16,1152]{2,1,0:T(8,128)(2,1)}), bf16[8,16,1152]{2,1,0:T(8,128)(2,1)S(1)}, u32[]{:S(2)}, u32[]{:S(2)}) async-start(bf16[8,16,1152]{2,1,0:T(8,128)(2,1)} %bitcast.4), calls=%async_computation.1 | async-start | bytes 589824 | tf_op jit(solution)/shard_map/all_to_all | solution.py:231
  94.3 0.0 copy-done.3
  94.4 12.0 %all-to-all-done.1 = bf16[8,16,1152]{2,1,0:T(8,128)(2,1)S(1)} async-done(((bf16[8,16,1152]{2,1,0:T(8,128)(2,1)}), bf16[8,16,1152]{2,1,0:T(8,128)(2,1)S(1)}, u32[]{:S(2)}, u32[]{:S(2)}) %all-to-all-start.1) | async-done | bytes 294944 | tf_op jit(solution)/shard_map/all_to_all | solution.py:231
  106.4 0.0 copy-done
  106.4 0.0 copy-done.1
  106.4 0.0 copy-done.2
  106.4 1.3 adam.1
  107.7 3.4 %all-to-all-start.2 = ((bf16[8,16,640]{2,1,0:T(8,128)(2,1)}), bf16[8,16,640]{2,1,0:T(8,128)(2,1)S(1)}, u32[]{:S(2)}, u32[]{:S(2)}) async-start(bf16[8,16,640]{2,1,0:T(8,128)(2,1)} %bitcast.6), calls=%async_computation.2 | async-start | bytes 327680 | tf_op jit(solution)/shard_map/all_to_all | solution.py:237
  111.1 28.5 %all_gather.3 = bf16[128,3968]{1,0:T(8,128)(2,1)S(1)} all-gather(bf16[16,3968]{1,0:T(8,128)(2,1)S(1)} %get-tuple-element.7), channel_id=1, replica_groups=mesh['vocab'=64,'two'=2,'four'=4] {'two','four'}, dimensions={0}, use_global_device_ids=true | all-gather | bytes 1142784 | tf_op jit(solution)/shard_map/all_gather | solution.py:236
  139.6 0.0 all-to-all-done.2
  139.6 1.1 pad_maximum_fusion
  (1 shorter events, 0.0 us)
Async XLA Ops:
  87.6 6.7 %copy-start.3 = (f32[4608]{0:T(1024)S(1)}, f32[4608]{0:T(1024)}, u32[]{:S(2)}) copy-start(f32[4608]{0:T(1024)} %param.9) | copy-start | bytes 55300
  87.6 18.7 %copy-start = (bf16[128,4608]{1,0:T(8,128)(2,1)S(1)}, bf16[128,4608]{1,0:T(8,128)(2,1)}, u32[]{:S(2)}) copy-start(bf16[128,4608]{1,0:T(8,128)(2,1)} %table_ref.1) | copy-start | bytes 3538948
  87.6 18.7 %copy-start.1 = (f32[16,4608]{1,0:T(8,128)S(1)}, f32[16,4608]{1,0:T(8,128)}, u32[]{:S(2)}) copy-start(f32[16,4608]{1,0:T(8,128)} %one_ref.1) | copy-start | bytes 884740
  87.6 18.8 %copy-start.2 = (f32[16,4608]{1,0:T(8,128)S(1)}, f32[16,4608]{1,0:T(8,128)}, u32[]{:S(2)}) copy-start(f32[16,4608]{1,0:T(8,128)} %two_ref.1) | copy-start | bytes 884740
  89.9 16.5 %all-to-all-start.1 = ((bf16[8,16,1152]{2,1,0:T(8,128)(2,1)}), bf16[8,16,1152]{2,1,0:T(8,128)(2,1)S(1)}, u32[]{:S(2)}, u32[]{:S(2)}) async-start(bf16[8,16,1152]{2,1,0:T(8,128)(2,1)} %bitcast.4), calls=%async_computation.1 | async-start | bytes 589824 | tf_op jit(solution)/shard_map/all_to_all | solution.py:231
  107.7 31.9 %all-to-all-start.2 = ((bf16[8,16,640]{2,1,0:T(8,128)(2,1)}), bf16[8,16,640]{2,1,0:T(8,128)(2,1)S(1)}, u32[]{:S(2)}, u32[]{:S(2)}) async-start(bf16[8,16,640]{2,1,0:T(8,128)(2,1)} %bitcast.6), calls=%async_computation.2 | async-start | bytes 327680 | tf_op jit(solution)/shard_map/all_to_all | solution.py:237

commit v7 on v6

--- a/solution.py
+++ b/solution.py
@@ -125,9 +125,7 @@
     picks = (found[: 2 * LANES].reshape(2, LANES, -1) * found[2 * LANES :][None]).reshape(
         2 * LANES, -1
     )
-    sums = jnp.dot(
-        picks.astype(jnp.bfloat16), part_ref[...], preferred_element_type=jnp.float32
-    ).astype(jnp.bfloat16)
+    sums = jnp.dot(picks.astype(jnp.bfloat16), part_ref[...], preferred_element_type=jnp.float32)
     out_ref[:, :piece] = sums[:LANES, :piece]
     out_ref[:, piece:] = sums[LANES:, :piece]
 
@@ -139,11 +137,11 @@
         collect_body,
         in_specs=[pl.BlockSpec(memory_space=pltpu.VMEM)],
         out_specs=pl.BlockSpec(memory_space=pltpu.VMEM),
-        out_shape=jax.ShapeDtypeStruct((LANES, 2 * piece), jnp.bfloat16),
+        out_shape=jax.ShapeDtypeStruct((LANES, 2 * piece), jnp.float32),
         compiler_params=pltpu.CompilerParams(vmem_limit_bytes=40 * 1024 * 1024),
         cost_estimate=pl.CostEstimate(
             flops=2 * count * 2 * LANES * lanes,
-            bytes_accessed=2 * (count * lanes + 2 * LANES * piece),
+            bytes_accessed=2 * count * lanes + 8 * LANES * piece,
             transcendentals=0,
         ),
         name="collect",
@@ -158,9 +156,9 @@
     rows = table_ref.shape[0]
     totals = []
     for member in range(MEMBERS):
-        total = sum_ref[member * rows : (member + 1) * rows, :].astype(jnp.float32)
+        total = sum_ref[member * rows : (member + 1) * rows, :]
         for peer in range(member + MEMBERS, sum_ref.shape[0] // rows, MEMBERS):
-            total = total + sum_ref[peer * rows : (peer + 1) * rows, :].astype(jnp.float32)
+            total = total + sum_ref[peer * rows : (peer + 1) * rows, :]
         totals.append(total)
     weighted = jnp.concatenate(totals, axis=1) * gain_ref[...]
     mean_square = jnp.mean(scaled * scaled, axis=-1, keepdims=True)

time: 143 us -> 150 us (1.049)
  waiting for transfers between devices: 12 us -> 18.4 us
    all_to_all x1, waiting for transfers between devices: 12 us -> 18.4 us  [on_device(): lax.all_to_all(row_sum, REP, split_axis=0, concat_axis=0, tiled=True)]
where the time goes in v7:
time: 150 us; the launch traced here: 148 us
  blocking collectives  112 us (75%)
  waiting for transfers between devices  18.4 us (12%)
  starting transfers between devices  7.93 us (5%)
  Pallas kernels  7.59 us (5%)
    all_to_all x1, blocking collectives, on_device(): lax.all_to_all(outgoing, ('vocab', 'four'), split_axis=0, concat_axis=0,...  83.1 us
    all_gather x1, blocking collectives, on_device(): left = lax.all_gather(updated, REP, axis=0, tiled=True)  29 us
    all_to_all x1, waiting for transfers between devices, on_device(): lax.all_to_all(row_sum, REP, split_axis=0, concat_axis=0, tiled=True)  18.4 us
    all_to_all x1, starting transfers between devices, on_device(): lax.all_to_all(row_sum, REP, split_axis=0, concat_axis=0, tiled=True)  4.55 us
    pallas_call x1, Pallas kernels, pack(): pl.pallas_call(pack_body, in_specs=[pl.BlockSpec(memory_space=pl.ANY), pl...  3.94 us
    all_to_all x1, starting transfers between devices, on_device(): right = lax.all_to_all(rest, REP, split_axis=0, concat_axis=0, tiled=True)  3.38 us
  transfers between devices with their start and end apart: 2, of which 1 were waited for; matrix products, arithmetic and copies ran while one was open for 0% of the time, Pallas kernels for 0%

profile of v7, /device:TPU:6, one launch (start us, length us, event | category | flops | bytes accessed | tf_op | source)
XLA Modules:
  0.0 147.7 jit_solution(4570220717710284873)
XLA Ops:
  0.6 3.9 %pack.1 = bf16[64,4,8,640]{3,2,1,0:T(8,128)(2,1)} custom-call(s32[1,128]{1,0:T(1,128)} %bitcast.12, bf16[128,4608]{1,0:T(8,128)(2,1)} %cot_hbm.1), custom_call_target="tpu_custom_call" | custom-call | flops 671088640 | bytes 3801088 | tf_op jit(solution)/shard_map/pack/pallas_call | solution.py:87
  4.6 83.1 %all_to_all.34 = bf16[256,8,640]{2,1,0:T(8,128)(2,1)S(1)} all-to-all(bf16[256,8,640]{2,1,0:T(8,128)(2,1)} %bitcast.10), channel_id=1, replica_groups=mesh['vocab'=64,'two'=2,'four'=4] {'vocab','four'}, dimensions={0} | all-to-all | bytes 5242880 | tf_op jit(solution)/shard_map/all_to_all | solution.py:227
  87.6 0.0 copy-start.3
  87.6 0.0 copy-start.1
  87.6 0.0 copy-start.2
  87.6 2.4 %collect.1 = f32[128,1152]{1,0:T(8,128)} custom-call(bf16[2048,640]{1,0:T(8,128)(2,1)S(1)} %bitcast.8), custom_call_target="tpu_custom_call" | custom-call | flops 671088640 | bytes 3211264 | tf_op jit(solution)/shard_map/collect/pallas_call | solution.py:136
  90.0 0.0 copy-start
  90.0 4.5 %all-to-all-start.1 = ((f32[8,16,1152]{2,1,0:T(8,128)}), f32[8,16,1152]{2,1,0:T(8,128)S(1)}, u32[]{:S(2)}, u32[]{:S(2)}) async-start(f32[8,16,1152]{2,1,0:T(8,128)} %bitcast.4), calls=%async_computation.1 | async-start | bytes 1179648 | tf_op jit(solution)/shard_map/all_to_all | solution.py:229
  94.5 0.0 copy-done.3
  94.6 18.4 %all-to-all-done.1 = f32[8,16,1152]{2,1,0:T(8,128)S(1)} async-done(((f32[8,16,1152]{2,1,0:T(8,128)}), f32[8,16,1152]{2,1,0:T(8,128)S(1)}, u32[]{:S(2)}, u32[]{:S(2)}) %all-to-all-start.1) | async-done | bytes 589856 | tf_op jit(solution)/shard_map/all_to_all | solution.py:229
  112.9 0.0 copy-done.1
  112.9 0.0 copy-done.2
  112.9 0.0 copy-done
  112.9 1.3 adam.1
  114.2 3.4 %all-to-all-start.2 = ((bf16[8,16,640]{2,1,0:T(8,128)(2,1)}), bf16[8,16,640]{2,1,0:T(8,128)(2,1)S(1)}, u32[]{:S(2)}, u32[]{:S(2)}) async-start(bf16[8,16,640]{2,1,0:T(8,128)(2,1)} %bitcast.6), calls=%async_computation.2 | async-start | bytes 327680 | tf_op jit(solution)/shard_map/all_to_all | solution.py:235
  117.6 29.0 %all_gather.3 = bf16[128,3968]{1,0:T(8,128)(2,1)S(1)} all-gather(bf16[16,3968]{1,0:T(8,128)(2,1)S(1)} %get-tuple-element.7), channel_id=1, replica_groups=mesh['vocab'=64,'two'=2,'four'=4] {'two','four'}, dimensions={0}, use_global_device_ids=true | all-gather | bytes 1142784 | tf_op jit(solution)/shard_map/all_gather | solution.py:234
  146.6 0.0 all-to-all-done.2
  146.6 1.1 pad_maximum_fusion
  (1 shorter events, 0.0 us)
Async XLA Ops:
  87.6 6.9 %copy-start.3 = (f32[4608]{0:T(1024)S(1)}, f32[4608]{0:T(1024)}, u32[]{:S(2)}) copy-start(f32[4608]{0:T(1024)} %param.9) | copy-start | bytes 55300
  87.6 25.3 %copy-start.1 = (f32[16,4608]{1,0:T(8,128)S(1)}, f32[16,4608]{1,0:T(8,128)}, u32[]{:S(2)}) copy-start(f32[16,4608]{1,0:T(8,128)} %one_ref.1) | copy-start | bytes 884740
  87.6 25.3 %copy-start.2 = (f32[16,4608]{1,0:T(8,128)S(1)}, f32[16,4608]{1,0:T(8,128)}, u32[]{:S(2)}) copy-start(f32[16,4608]{1,0:T(8,128)} %two_ref.1) | copy-start | bytes 884740
  90.0 22.9 %copy-start = (bf16[128,4608]{1,0:T(8,128)(2,1)S(1)}, bf16[128,4608]{1,0:T(8,128)(2,1)}, u32[]{:S(2)}) copy-start(bf16[128,4608]{1,0:T(8,128)(2,1)} %table_ref.1) | copy-start | bytes 3538948
  90.0 22.9 %all-to-all-start.1 = ((f32[8,16,1152]{2,1,0:T(8,128)}), f32[8,16,1152]{2,1,0:T(8,128)S(1)}, u32[]{:S(2)}, u32[]{:S(2)}) async-start(f32[8,16,1152]{2,1,0:T(8,128)} %bitcast.4), calls=%async_computation.1 | async-start | bytes 1179648 | tf_op jit(solution)/shard_map/all_to_all | solution.py:229
  114.2 32.3 %all-to-all-start.2 = ((bf16[8,16,640]{2,1,0:T(8,128)(2,1)}), bf16[8,16,640]{2,1,0:T(8,128)(2,1)S(1)}, u32[]{:S(2)}, u32[]{:S(2)}) async-start(bf16[8,16,640]{2,1,0:T(8,128)(2,1)} %bitcast.6), calls=%async_computation.2 | async-start | bytes 327680 | tf_op jit(solution)/shard_map/all_to_all | solution.py:235

commit v8 on v6

--- a/solution.py
+++ b/solution.py
@@ -19,7 +19,6 @@
 
 SLOTS = 4
 LANES = 128
-GATHERED = 3968
 MEMBERS = 4
 HIGH = 8
 LOW = 16
@@ -150,7 +149,7 @@
     )(arrived)
 
 
-def adam_body(rep_ref, sum_ref, table_ref, gain_ref, one_ref, two_ref, up_ref, rest_ref, one_out, two_out):
+def adam_body(rep_ref, sum_ref, table_ref, gain_ref, one_ref, two_ref, up_ref, one_out, two_out):
     width = table_ref.shape[1]
     root = math.sqrt(width)
     params = table_ref[...].astype(jnp.float32)
@@ -174,11 +173,7 @@
     update = (
         new_one / correct_one / (jnp.sqrt(new_two / correct_two) + adam_eps) + decay_rate * params
     )
-    updated = (params - learn_rate * update).astype(jnp.bfloat16)
-    up_ref[...] = updated[:, :GATHERED]
-    rest = updated[:, GATHERED:]
-    for peer in range(rest_ref.shape[0] // rows):
-        rest_ref[peer * rows : (peer + 1) * rows, :] = rest
+    up_ref[...] = (params - learn_rate * update).astype(jnp.bfloat16)
 
 
 def adam(rep_index, partial_sums, embed_table, norm_gain, moment_one, moment_two):
@@ -197,16 +192,10 @@
                 whole,
                 whole,
             ],
-            out_specs=[
-                pl.BlockSpec((rows, GATHERED), lambda i, rep: (0, 0)),
-                pl.BlockSpec((peers * rows, width - GATHERED), lambda i, rep: (0, 0)),
-                whole,
-                whole,
-            ],
+            out_specs=[whole, whole, whole],
         ),
         out_shape=[
-            jax.ShapeDtypeStruct((rows, GATHERED), jnp.bfloat16),
-            jax.ShapeDtypeStruct((peers * rows, width - GATHERED), jnp.bfloat16),
+            jax.ShapeDtypeStruct((rows, width), jnp.bfloat16),
             jax.ShapeDtypeStruct((rows, width), jnp.float32),
             jax.ShapeDtypeStruct((rows, width), jnp.float32),
         ],
@@ -218,30 +207,70 @@
     )(rep_index, partial_sums, embed_table, norm_gain.reshape(1, width), moment_one, moment_two)
 
 
-REP = ("two", "four")
-ALL = ("vocab", "two", "four")
+def place_body(side_ref, mine_ref, others_ref, out_hbm, sems):
+    count, rows, _ = mine_ref.shape
+    side = side_ref[0]
+    copies = []
+    for at in range(count):
+        for which, source in enumerate((mine_ref, others_ref)):
+            parity = side if which == 0 else 1 - side
+            start = pl.multiple_of((2 * at + parity) * rows, rows)
+            copies.append(
+                pltpu.make_async_copy(
+                    source.at[at], out_hbm.at[pl.ds(start, rows), :], sems.at[2 * at + which]
+                )
+            )
+    for copy in copies:
+        copy.start()
+    for copy in copies:
+        copy.wait()
+
+
+def place(side, mine, others):
+    count, rows, width = mine.shape
+    return pl.pallas_call(
+        place_body,
+        in_specs=[
+            pl.BlockSpec(memory_space=pltpu.SMEM),
+            pl.BlockSpec(memory_space=pltpu.VMEM),
+            pl.BlockSpec(memory_space=pltpu.VMEM),
+        ],
+        out_specs=pl.BlockSpec(memory_space=pl.ANY),
+        out_shape=jax.ShapeDtypeStruct((2 * count * rows, width), mine.dtype),
+        scratch_shapes=[pltpu.SemaphoreType.DMA((2 * count,))],
+        compiler_params=pltpu.CompilerParams(vmem_limit_bytes=24 * 1024 * 1024),
+        cost_estimate=pl.CostEstimate(
+            flops=0, bytes_accessed=8 * count * rows * width, transcendentals=0
+        ),
+        name="place",
+    )(side, mine, others)
+
+
+REP = ("far", "near", "side")
+ALL = ("vocab", "far", "near", "side")
 
 
 def on_device(token_ids, cotangent, embed_table, norm_gain, moment_one, moment_two):
     peer_count = lax.axis_size("vocab")
     outgoing = pack(token_ids, cotangent, peer_count)
     outgoing = outgoing.reshape(-1, outgoing.shape[-1])
-    arrived = lax.all_to_all(outgoing, ("vocab", "four"), split_axis=0, concat_axis=0, tiled=True)
+    arrived = lax.all_to_all(outgoing, ("vocab", "near", "side"), split_axis=0, concat_axis=0, tiled=True)
     row_sum = collect(arrived)
     partial_sums = lax.all_to_all(row_sum, REP, split_axis=0, concat_axis=0, tiled=True)
     rep_index = lax.axis_index(REP).astype(jnp.int32).reshape(1)
-    updated, rest, new_moment_one, new_moment_two = adam(
+    updated, new_moment_one, new_moment_two = adam(
         rep_index, partial_sums, embed_table, norm_gain, moment_one, moment_two
     )
-    left = lax.all_gather(updated, REP, axis=0, tiled=True)
-    right = lax.all_to_all(rest, REP, split_axis=0, concat_axis=0, tiled=True)
-    new_table = jnp.concatenate([left, right], axis=1)
+    mine = lax.all_gather(updated, ("far", "near"), axis=0, tiled=False)
+    others = lax.ppermute(mine, "side", [(0, 1), (1, 0)])
+    side = lax.axis_index("side").astype(jnp.int32).reshape(1)
+    new_table = place(side, mine, others)
     return (new_table, new_moment_one, new_moment_two)
 
 
 def solution(mesh):
     vocab, rep = mesh.devices.shape
-    fours = Mesh(mesh.devices.reshape(vocab, rep // MEMBERS, MEMBERS), ALL)
+    fours = Mesh(mesh.devices.reshape(vocab, rep // MEMBERS, MEMBERS // 2, 2), ALL)
     placed = (
         P(ALL),
         P(ALL, None),

time: 143 us -> 140 us (0.979)
  blocking collectives: 112 us -> 99.2 us
  waiting for transfers between devices: 12 us -> 22.7 us
    all_gather x1, blocking collectives: 28.5 us -> 16.2 us  [on_device(): mine = lax.all_gather(updated, ('far', 'near'), axis=0, tiled=False)]
    ppermute x0 -> x1, waiting for transfers between devices: none -> 10.6 us  [on_device(): others = lax.ppermute(mine, 'side', [(0, 1), (1, 0)])]
    all_to_all x1 -> x0, starting transfers between devices: 3.38 us -> none  [on_device(): right = lax.all_to_all(rest, REP, split_axis=0, concat_axis=0, tiled=True)]
    ppermute x0 -> x1, starting transfers between devices: none -> 2.32 us  [on_device(): others = lax.ppermute(mine, 'side', [(0, 1), (1, 0)])]
  transfers between devices with their start and end apart: 2 -> 2, of which waited for: 1 -> 2; matrix products, arithmetic and copies ran while one was open for 0% -> 0% of each run, Pallas kernels for 0% -> 0%
where the time goes in v8:
time: 140 us; the launch traced here: 138 us
  blocking collectives  99.2 us (71%)
  waiting for transfers between devices  22.7 us (16%)
  Pallas kernels  8.35 us (6%)
  starting transfers between devices  6.73 us (5%)
    all_to_all x1, blocking collectives, on_device(): lax.all_to_all(outgoing, ('vocab', 'near', 'side'), split_axis=0, concat_...  83.1 us
    all_gather x1, blocking collectives, on_device(): mine = lax.all_gather(updated, ('far', 'near'), axis=0, tiled=False)  16.2 us
    all_to_all x1, waiting for transfers between devices, on_device(): lax.all_to_all(row_sum, REP, split_axis=0, concat_axis=0, tiled=True)  12 us
    ppermute x1, waiting for transfers between devices, on_device(): others = lax.ppermute(mine, 'side', [(0, 1), (1, 0)])  10.6 us
    all_to_all x1, starting transfers between devices, on_device(): lax.all_to_all(row_sum, REP, split_axis=0, concat_axis=0, tiled=True)  4.42 us
    pallas_call x1, Pallas kernels, pack(): pl.pallas_call(pack_body, in_specs=[pl.BlockSpec(memory_space=pl.ANY), pl...  3.92 us
  transfers between devices with their start and end apart: 2, of which 2 were waited for; matrix products, arithmetic and copies ran while one was open for 0% of the time, Pallas kernels for 0%

profile of v8, /device:TPU:6, one launch (start us, length us, event | category | flops | bytes accessed | tf_op | source)
XLA Modules:
  0.0 137.7 jit_solution(759209470566335126)
XLA Ops:
  0.6 3.9 %pack.1 = bf16[64,4,8,640]{3,2,1,0:T(8,128)(2,1)} custom-call(s32[1,128]{1,0:T(1,128)} %bitcast.13, bf16[128,4608]{1,0:T(8,128)(2,1)} %cot_hbm.1), custom_call_target="tpu_custom_call" | custom-call | flops 671088640 | bytes 3801088 | tf_op jit(solution)/shard_map/pack/pallas_call | solution.py:86
  4.6 83.1 %all_to_all.22 = bf16[256,8,640]{2,1,0:T(8,128)(2,1)S(1)} all-to-all(bf16[256,8,640]{2,1,0:T(8,128)(2,1)} %bitcast.12), channel_id=1, replica_groups=mesh['vocab'=64,'far'=2,'near'=2,'side'=2] {'vocab','near','side'}, dimensions={0} | all-to-all | bytes 5242880 | tf_op jit(solution)/shard_map/all_to_all | solution.py:257
  87.6 0.0 copy-start.3
  87.6 0.0 copy-start
  87.6 0.0 copy-start.1
  87.6 0.0 copy-start.2
  87.6 2.3 %collect.1 = bf16[128,1152]{1,0:T(8,128)(2,1)} custom-call(bf16[2048,640]{1,0:T(8,128)(2,1)S(1)} %bitcast.8), custom_call_target="tpu_custom_call" | custom-call | flops 671088640 | bytes 2916352 | tf_op jit(solution)/shard_map/collect/pallas_call | solution.py:137
  89.9 4.4 %all-to-all-start.1 = ((bf16[8,16,1152]{2,1,0:T(8,128)(2,1)}), bf16[8,16,1152]{2,1,0:T(8,128)(2,1)S(1)}, u32[]{:S(2)}, u32[]{:S(2)}) async-start(bf16[8,16,1152]{2,1,0:T(8,128)(2,1)} %bitcast.5), calls=%async_computation.1 | async-start | bytes 589824 | tf_op jit(solution)/shard_map/all_to_all | solution.py:259
  94.3 0.0 copy-done.3
  94.3 12.0 %all-to-all-done.1 = bf16[8,16,1152]{2,1,0:T(8,128)(2,1)S(1)} async-done(((bf16[8,16,1152]{2,1,0:T(8,128)(2,1)}), bf16[8,16,1152]{2,1,0:T(8,128)(2,1)S(1)}, u32[]{:S(2)}, u32[]{:S(2)}) %all-to-all-start.1) | async-done | bytes 294944 | tf_op jit(solution)/shard_map/all_to_all | solution.py:259
  106.4 0.0 copy-done
  106.4 0.0 copy-done.1
  106.4 0.0 copy-done.2
  106.4 1.1 adam.1
  107.5 16.2 %all-gather = bf16[64,4608]{1,0:T(8,128)(2,1)S(1)} all-gather(bf16[16,4608]{1,0:T(8,128)(2,1)S(1)} %get-tuple-element.6), channel_id=2, replica_groups=mesh['vocab'=64,'far'=2,'near'=2,'side'=2] {'far','near'}, dimensions={0}, use_global_device_ids=true | all-gather | bytes 737280 | tf_op jit(solution)/shard_map/all_gather | solution.py:264
  123.6 2.3 %collective-permute-start = (bf16[4,16,4608]{2,1,0:T(8,128)(2,1)S(1)}, bf16[4,16,4608]{2,1,0:T(8,128)(2,1)S(1)}, u32[]{:S(2)}, u32[]{:S(2)}) collective-permute-start(bf16[4,16,4608]{2,1,0:T(8,128)(2,1)S(1)} %bitcast.9), channel_id=1, source_target_pairs={{0,1},{1,0},{2,3},{3,2},{4,5},{5,4},{6,7},{7,6},{8,9},{9,8},{10,11... | collective-permute-start | bytes 1769480 | tf_op jit(solution)/shard_map/ppermute | solution.py:265
  126.0 10.6 %collective-permute-done.others_ref = bf16[4,16,4608]{2,1,0:T(8,128)(2,1)S(1)} collective-permute-done((bf16[4,16,4608]{2,1,0:T(8,128)(2,1)S(1)}, bf16[4,16,4608]{2,1,0:T(8,128)(2,1)S(1)}, u32[]{:S(2)}, u32[]{:S(2)}) %collective-permute-start) | collective-permute-done | bytes 589856 | tf_op jit(solution)/shard_map/ppermute | solution.py:265
  136.6 1.1 place.1
  (1 shorter events, 0.0 us)
Async XLA Ops:
  87.6 6.7 %copy-start.3 = (f32[4608]{0:T(1024)S(1)}, f32[4608]{0:T(1024)}, u32[]{:S(2)}) copy-start(f32[4608]{0:T(1024)} %param.9) | copy-start | bytes 55300
  87.6 18.7 %copy-start = (bf16[128,4608]{1,0:T(8,128)(2,1)S(1)}, bf16[128,4608]{1,0:T(8,128)(2,1)}, u32[]{:S(2)}) copy-start(bf16[128,4608]{1,0:T(8,128)(2,1)} %table_ref.1) | copy-start | bytes 3538948
  87.6 18.8 %copy-start.1 = (f32[16,4608]{1,0:T(8,128)S(1)}, f32[16,4608]{1,0:T(8,128)}, u32[]{:S(2)}) copy-start(f32[16,4608]{1,0:T(8,128)} %one_ref.1) | copy-start | bytes 884740
  87.6 18.8 %copy-start.2 = (f32[16,4608]{1,0:T(8,128)S(1)}, f32[16,4608]{1,0:T(8,128)}, u32[]{:S(2)}) copy-start(f32[16,4608]{1,0:T(8,128)} %two_ref.1) | copy-start | bytes 884740
  89.9 16.5 %all-to-all-start.1 = ((bf16[8,16,1152]{2,1,0:T(8,128)(2,1)}), bf16[8,16,1152]{2,1,0:T(8,128)(2,1)S(1)}, u32[]{:S(2)}, u32[]{:S(2)}) async-start(bf16[8,16,1152]{2,1,0:T(8,128)(2,1)} %bitcast.5), calls=%async_computation.1 | async-start | bytes 589824 | tf_op jit(solution)/shard_map/all_to_all | solution.py:259
  123.6 13.0 %collective-permute-start = (bf16[4,16,4608]{2,1,0:T(8,128)(2,1)S(1)}, bf16[4,16,4608]{2,1,0:T(8,128)(2,1)S(1)}, u32[]{:S(2)}, u32[]{:S(2)}) collective-permute-start(bf16[4,16,4608]{2,1,0:T(8,128)(2,1)S(1)} %bitcast.9), channel_id=1, source_target_pairs={{0,1},{1,0},{2,3},{3,2},{4,5},{5,4},{6,7},{7,6},{8,9},{9,8},{10,11... | collective-permute-start | bytes 1769480 | tf_op jit(solution)/shard_map/ppermute | solution.py:265

commit v9 on v8

--- a/solution.py
+++ b/solution.py
@@ -54,22 +54,22 @@
     rows = lax.broadcasted_iota(jnp.int32, (owners * per_owner, 2 * tok_count), 0)
     picks = (rows == slots).astype(jnp.bfloat16)
     high = (ids_down >> 4) & (HIGH - 1)
-    low = (ids_down & (LOW - 1)) + 2 * HIGH
+    low = (ids_down & (LOW - 1)) + HIGH
     marks = [
-        ((along == high + half * HIGH) | (along == low)).astype(jnp.bfloat16)[:, : lanes - piece]
-        for half in range(2)
+        ((along == high + at) | (along == low + at)).astype(jnp.float32) for at in (CODE, 0)
     ]
-    for member in range(MEMBERS):
-        for half in range(2):
-            piece_ref[member, half * tok_count : (half + 1) * tok_count, piece:] = marks[half]
+    body = piece + CODE - LANES
     sends = []
     for member in range(MEMBERS):
         copies[member].wait()
+        shared = cot_ref[:, (member + 1) * own - LANES : (member + 1) * own].astype(jnp.float32)
         for half in range(2):
-            at = member * own + half * piece
-            piece_ref[member, half * tok_count : (half + 1) * tok_count, :piece] = cot_ref[
-                :, at : at + piece
-            ]
+            at = member * own + half * body
+            rows_of = slice(half * tok_count, (half + 1) * tok_count)
+            piece_ref[member, rows_of, :body] = cot_ref[:, at : at + body]
+            piece_ref[member, rows_of, body:] = jnp.where(
+                (along < CODE) == (half == 0), shared, marks[half]
+            ).astype(jnp.bfloat16)
         moved = jnp.dot(picks, piece_ref[member], preferred_element_type=jnp.float32)
         out_ref[member] = moved.reshape(owners, per_owner, lanes).astype(jnp.bfloat16)
         sends.append(
@@ -107,28 +107,31 @@
 
 
 def collect_body(part_ref, out_ref):
-    piece = out_ref.shape[1] // 2
-    shard_row = lax.broadcasted_iota(jnp.int32, (LANES, CODE), 0)
-    lane = lax.broadcasted_iota(jnp.int32, (LANES, CODE), 1)
+    body = part_ref.shape[1] - LANES
+    shard_row = lax.broadcasted_iota(jnp.int32, (LANES, LANES), 0)
+    lane = lax.broadcasted_iota(jnp.int32, (LANES, LANES), 1)
     high = shard_row >> 4
-    low = (shard_row & (LOW - 1)) + 2 * HIGH
+    low = (shard_row & (LOW - 1)) + HIGH
     digits = jnp.concatenate(
-        [(lane == value).astype(jnp.bfloat16) for value in (high, high + HIGH, low)], axis=0
+        [(lane == value).astype(jnp.bfloat16) for value in (high + CODE, high, low + CODE, low)],
+        axis=0,
     )
     found = lax.dot_general(
         digits,
-        part_ref[:, piece:],
+        part_ref[:, body:],
         (((1,), (1,)), ((), ())),
         preferred_element_type=jnp.float32,
     )
-    picks = (found[: 2 * LANES].reshape(2, LANES, -1) * found[2 * LANES :][None]).reshape(
-        2 * LANES, -1
-    )
-    sums = jnp.dot(
-        picks.astype(jnp.bfloat16), part_ref[...], preferred_element_type=jnp.float32
-    ).astype(jnp.bfloat16)
-    out_ref[:, :piece] = sums[:LANES, :piece]
-    out_ref[:, piece:] = sums[LANES:, :piece]
+    half = lax.broadcasted_iota(jnp.int32, (LANES, found.shape[1]), 1) & SLOTS
+    first = jnp.where(half == 0, found[:LANES] * found[2 * LANES : 3 * LANES], 0.0)
+    second = jnp.where(half == 0, 0.0, found[LANES : 2 * LANES] * found[3 * LANES :])
+    picks = jnp.concatenate([first, second], axis=0).astype(jnp.bfloat16)
+    sums = jnp.dot(picks, part_ref[...], preferred_element_type=jnp.float32)
+    out_ref[:, :body] = sums[:LANES, :body].astype(jnp.bfloat16)
+    out_ref[:, body : 2 * body] = sums[LANES:, :body].astype(jnp.bfloat16)
+    out_ref[:, 2 * body :] = jnp.where(lane < CODE, sums[:LANES, body:], sums[LANES:, body:]).astype(
+        jnp.bfloat16
+    )
 
 
 def collect(arrived):

time: 140 us -> 139 us (level)
  no operation moved by 1% of the time
where the time goes in v9:
time: 139 us; the launch traced here: 137 us
  blocking collectives  99.2 us (71%)
  waiting for transfers between devices  22.7 us (16%)
  Pallas kernels  8.07 us (6%)
  starting transfers between devices  6.73 us (5%)
    all_to_all x1, blocking collectives, on_device(): lax.all_to_all(outgoing, ('vocab', 'near', 'side'), split_axis=0, concat_...  83.1 us
    all_gather x1, blocking collectives, on_device(): mine = lax.all_gather(updated, ('far', 'near'), axis=0, tiled=False)  16.2 us
    all_to_all x1, waiting for transfers between devices, on_device(): lax.all_to_all(row_sum, REP, split_axis=0, concat_axis=0, tiled=True)  12 us
    ppermute x1, waiting for transfers between devices, on_device(): others = lax.ppermute(mine, 'side', [(0, 1), (1, 0)])  10.6 us
    all_to_all x1, starting transfers between devices, on_device(): lax.all_to_all(row_sum, REP, split_axis=0, concat_axis=0, tiled=True)  4.41 us
    pallas_call x1, Pallas kernels, pack(): pl.pallas_call(pack_body, in_specs=[pl.BlockSpec(memory_space=pl.ANY), pl...  3.65 us
  transfers between devices with their start and end apart: 2, of which 2 were waited for; matrix products, arithmetic and copies ran while one was open for 0% of the time, Pallas kernels for 0%

profile of v9, /device:TPU:6, one launch (start us, length us, event | category | flops | bytes accessed | tf_op | source)
XLA Modules:
  0.0 137.4 jit_solution(17017732012013862953)
XLA Ops:
  0.6 3.7 %pack.1 = bf16[64,4,8,640]{3,2,1,0:T(8,128)(2,1)} custom-call(s32[1,128]{1,0:T(1,128)} %bitcast.13, bf16[128,4608]{1,0:T(8,128)(2,1)} %cot_hbm.1), custom_call_target="tpu_custom_call" | custom-call | flops 671088640 | bytes 3801088 | tf_op jit(solution)/shard_map/pack/pallas_call | solution.py:86
  4.3 83.1 %all_to_all.22 = bf16[256,8,640]{2,1,0:T(8,128)(2,1)S(1)} all-to-all(bf16[256,8,640]{2,1,0:T(8,128)(2,1)} %bitcast.12), channel_id=1, replica_groups=mesh['vocab'=64,'far'=2,'near'=2,'side'=2] {'vocab','near','side'}, dimensions={0} | all-to-all | bytes 5242880 | tf_op jit(solution)/shard_map/all_to_all | solution.py:260
  87.3 0.0 copy-start.3
  87.3 0.0 copy-start
  87.3 0.0 copy-start.1
  87.3 0.0 copy-start.2
  87.4 2.2 %collect.1 = bf16[128,1152]{1,0:T(8,128)(2,1)} custom-call(bf16[2048,640]{1,0:T(8,128)(2,1)S(1)} %bitcast.8), custom_call_target="tpu_custom_call" | custom-call | flops 671088640 | bytes 2916352 | tf_op jit(solution)/shard_map/collect/pallas_call | solution.py:140
  89.6 4.4 %all-to-all-start.1 = ((bf16[8,16,1152]{2,1,0:T(8,128)(2,1)}), bf16[8,16,1152]{2,1,0:T(8,128)(2,1)S(1)}, u32[]{:S(2)}, u32[]{:S(2)}) async-start(bf16[8,16,1152]{2,1,0:T(8,128)(2,1)} %bitcast.5), calls=%async_computation.1 | async-start | bytes 589824 | tf_op jit(solution)/shard_map/all_to_all | solution.py:262
  94.0 0.0 copy-done.3
  94.0 12.0 %all-to-all-done.1 = bf16[8,16,1152]{2,1,0:T(8,128)(2,1)S(1)} async-done(((bf16[8,16,1152]{2,1,0:T(8,128)(2,1)}), bf16[8,16,1152]{2,1,0:T(8,128)(2,1)S(1)}, u32[]{:S(2)}, u32[]{:S(2)}) %all-to-all-start.1) | async-done | bytes 294944 | tf_op jit(solution)/shard_map/all_to_all | solution.py:262
  106.1 0.0 copy-done
  106.1 0.0 copy-done.1
  106.1 0.0 copy-done.2
  106.1 1.1 adam.1
  107.2 16.2 %all-gather = bf16[64,4608]{1,0:T(8,128)(2,1)S(1)} all-gather(bf16[16,4608]{1,0:T(8,128)(2,1)S(1)} %get-tuple-element.6), channel_id=2, replica_groups=mesh['vocab'=64,'far'=2,'near'=2,'side'=2] {'far','near'}, dimensions={0}, use_global_device_ids=true | all-gather | bytes 737280 | tf_op jit(solution)/shard_map/all_gather | solution.py:267
  123.3 2.3 %collective-permute-start = (bf16[4,16,4608]{2,1,0:T(8,128)(2,1)S(1)}, bf16[4,16,4608]{2,1,0:T(8,128)(2,1)S(1)}, u32[]{:S(2)}, u32[]{:S(2)}) collective-permute-start(bf16[4,16,4608]{2,1,0:T(8,128)(2,1)S(1)} %bitcast.9), channel_id=1, source_target_pairs={{0,1},{1,0},{2,3},{3,2},{4,5},{5,4},{6,7},{7,6},{8,9},{9,8},{10,11... | collective-permute-start | bytes 1769480 | tf_op jit(solution)/shard_map/ppermute | solution.py:268
  125.7 10.6 %collective-permute-done.others_ref = bf16[4,16,4608]{2,1,0:T(8,128)(2,1)S(1)} collective-permute-done((bf16[4,16,4608]{2,1,0:T(8,128)(2,1)S(1)}, bf16[4,16,4608]{2,1,0:T(8,128)(2,1)S(1)}, u32[]{:S(2)}, u32[]{:S(2)}) %collective-permute-start) | collective-permute-done | bytes 589856 | tf_op jit(solution)/shard_map/ppermute | solution.py:268
  136.3 1.1 place.1
  (1 shorter events, 0.0 us)
Async XLA Ops:
  87.3 6.7 %copy-start.3 = (f32[4608]{0:T(1024)S(1)}, f32[4608]{0:T(1024)}, u32[]{:S(2)}) copy-start(f32[4608]{0:T(1024)} %param.9) | copy-start | bytes 55300
  87.3 18.7 %copy-start = (bf16[128,4608]{1,0:T(8,128)(2,1)S(1)}, bf16[128,4608]{1,0:T(8,128)(2,1)}, u32[]{:S(2)}) copy-start(bf16[128,4608]{1,0:T(8,128)(2,1)} %table_ref.1) | copy-start | bytes 3538948
  87.3 18.7 %copy-start.1 = (f32[16,4608]{1,0:T(8,128)S(1)}, f32[16,4608]{1,0:T(8,128)}, u32[]{:S(2)}) copy-start(f32[16,4608]{1,0:T(8,128)} %one_ref.1) | copy-start | bytes 884740
  87.3 18.7 %copy-start.2 = (f32[16,4608]{1,0:T(8,128)S(1)}, f32[16,4608]{1,0:T(8,128)}, u32[]{:S(2)}) copy-start(f32[16,4608]{1,0:T(8,128)} %two_ref.1) | copy-start | bytes 884740
  89.6 16.5 %all-to-all-start.1 = ((bf16[8,16,1152]{2,1,0:T(8,128)(2,1)}), bf16[8,16,1152]{2,1,0:T(8,128)(2,1)S(1)}, u32[]{:S(2)}, u32[]{:S(2)}) async-start(bf16[8,16,1152]{2,1,0:T(8,128)(2,1)} %bitcast.5), calls=%async_computation.1 | async-start | bytes 589824 | tf_op jit(solution)/shard_map/all_to_all | solution.py:262
  123.3 13.0 %collective-permute-start = (bf16[4,16,4608]{2,1,0:T(8,128)(2,1)S(1)}, bf16[4,16,4608]{2,1,0:T(8,128)(2,1)S(1)}, u32[]{:S(2)}, u32[]{:S(2)}) collective-permute-start(bf16[4,16,4608]{2,1,0:T(8,128)(2,1)S(1)} %bitcast.9), channel_id=1, source_target_pairs={{0,1},{1,0},{2,3},{3,2},{4,5},{5,4},{6,7},{7,6},{8,9},{9,8},{10,11... | collective-permute-start | bytes 1769480 | tf_op jit(solution)/shard_map/ppermute | solution.py:268
